TPU v7x, 32 devices: a whole 2x2x4 slice. The times are simulated.
32 devices in a mesh: event: 4 (over z), blk: 8 (over y, x, core).
Axes of the slice: x: 2, y: 2, z: 4, core: 2. Of those that a mesh axis runs over, the one named last changes fastest.
Arguments:
- features: bfloat16 [4, 192, 64, 512], P('event', 'blk'), may hold values from -6 to 6
- occupancy: int32 [4, 192, 512], P('event', 'blk'), may hold values 0 or 1
- block_cells: int32 [4, 192], P('event'), may hold values from 0 to 63, as said below
- weight: bfloat16 [27, 64, 64], replicated, may hold values from -0.15625 to 0.15625
- cotangent: bfloat16 [4, 192, 64, 512], P('event', 'blk'), may hold values from -6 to 6
Outputs:
- output: bfloat16 [4, 192, 64, 512], P('event', 'blk')
- grad_features: bfloat16 [4, 192, 64, 512], P('event', 'blk')
- grad_weight: float32 [27, 64, 64], replicated
Inputs may be any that keep to these rules, and one draw needn't show every extreme that they name: `block_cells`: blocks of an event are listed plane by plane, 24 to a plane, planes 0 to 7 in order; within a plane the cells are distinct and increasing. Index i of blk owns plane i.
All inputs are finite; a program needn't handle non-finite values. No bound on the sum of `occupancy` on one device may be relied on, other than what follows from the above.
Results may differ from a plain program's by a relative error of at most 0.001.
Values may be sent and summed in bfloat16 or wider, within the bound.
A program may use at most 128 MiB of HBM per device.

v0:
```python
import math

import jax
import jax.numpy as jnp
from jax import lax
from jax.sharding import PartitionSpec as P

CHANNELS = 64
EDGE = 8
VOXELS = 512
TAPS = 27
GRID_Y = 8
GRID_Z = 8
CELLS = 64
ACTIVE = 24


def shifted(x, axis, by):
    devices = lax.axis_size(axis)
    pairs = [(i, i + by) for i in range(devices) if 0 <= i + by < devices]
    return lax.ppermute(x, axis, pairs)


def offset_list():
    return [
        (step_x, step_y, step_z)
        for step_x in (-1, 0, 1)
        for step_y in (-1, 0, 1)
        for step_z in (-1, 0, 1)
    ]


def ranges_for(offset_step):
    if offset_step < 0:
        return (slice(0, 1), slice(EDGE - 1, EDGE))
    if offset_step > 0:
        return (slice(EDGE + 1, EDGE + 2), slice(0, 1))
    return (slice(1, EDGE + 1), slice(0, EDGE))


def neighbour_slots(own_plane, own_cells, table_gid, offset):
    row_y = own_cells // GRID_Z + offset[1]
    row_z = own_cells % GRID_Z + offset[2]
    inside = (row_y >= 0) & (row_y < GRID_Y) & (row_z >= 0) & (row_z < GRID_Z)
    target = (own_plane + offset[0]) * CELLS + row_y * GRID_Z + row_z
    matches = (target[:, None] == table_gid[None, :]) & inside[:, None]
    present = jnp.any(matches, axis=1)
    listing = jnp.arange(table_gid.shape[0], dtype=jnp.int32)[None, :]
    position = jnp.sum(jnp.where(matches, listing, 0), axis=1)
    return (present, position)


def build_padded(centre, table, own_plane, own_cells, table_gid):
    count = centre.shape[0]
    padded = jnp.zeros((count, CHANNELS, EDGE + 2, EDGE + 2, EDGE + 2), centre.dtype)
    padded = padded.at[:, :, 1 : EDGE + 1, 1 : EDGE + 1, 1 : EDGE + 1].set(centre)
    for offset in offset_list():
        if offset == (0, 0, 0):
            continue
        present, position = neighbour_slots(own_plane, own_cells, table_gid, offset)
        dest_x, source_x = ranges_for(offset[0])
        dest_y, source_y = ranges_for(offset[1])
        dest_z, source_z = ranges_for(offset[2])
        slab = table[:, :, source_x, source_y, source_z]
        picked = jnp.take(slab, position, axis=0)
        picked = jnp.where(present[:, None, None, None, None], picked, jnp.zeros_like(picked))
        padded = padded.at[:, :, dest_x, dest_y, dest_z].set(picked)
    return padded


def columns(padded, orient):
    pieces = []
    for offset in offset_list():
        starts = [1 + orient * offset_step for offset_step in offset]
        piece = padded[
            :,
            :,
            starts[0] : starts[0] + EDGE,
            starts[1] : starts[1] + EDGE,
            starts[2] : starts[2] + EDGE,
        ]
        pieces.append(piece.reshape(padded.shape[0], CHANNELS, VOXELS))
    return jnp.concatenate(pieces, axis=1)


def extended(local, below_face, above_face):
    empty = jnp.zeros((ACTIVE, CHANNELS, EDGE, EDGE, EDGE), jnp.bfloat16)
    below_block = empty.at[:, :, EDGE - 1].set(below_face.reshape(ACTIVE, CHANNELS, EDGE, EDGE))
    above_block = empty.at[:, :, 0].set(above_face.reshape(ACTIVE, CHANNELS, EDGE, EDGE))
    return jnp.concatenate([below_block, local, above_block], axis=0)


def per_device(features, occupancy, block_cells, weight, cotangent):
    device = lax.axis_index("blk")
    count = features.shape[1]
    plane_count = count // ACTIVE
    face_size = CHANNELS * EDGE * EDGE
    mask_half = occupancy[0].astype(jnp.bfloat16)
    masked = features[0] * mask_half[:, None, :]
    grad_masked = cotangent[0] * mask_half[:, None, :]
    volume = masked.reshape(count, CHANNELS, EDGE, EDGE, EDGE)
    grad_volume = grad_masked.reshape(count, CHANNELS, EDGE, EDGE, EDGE)
    paired = jnp.stack([volume, grad_volume])
    low_faces = paired[:, :ACTIVE, :, 0].reshape(2, ACTIVE, face_size)
    high_faces = paired[:, count - ACTIVE :, :, EDGE - 1].reshape(2, ACTIVE, face_size)
    from_below = shifted(high_faces, "blk", 1)
    from_above = shifted(low_faces, "blk", -1)
    filler = jnp.full((ACTIVE,), -1, jnp.int32)
    padded_cells = jnp.concatenate([filler, block_cells[0], filler])
    cells_ext = lax.dynamic_slice_in_dim(padded_cells, device * count, (plane_count + 2) * ACTIVE)
    ext_plane = jnp.arange((plane_count + 2) * ACTIVE, dtype=jnp.int32) // ACTIVE
    table_gid = jnp.where(cells_ext >= 0, ext_plane * CELLS + cells_ext, -5)
    own_cells = cells_ext[ACTIVE : ACTIVE + count]
    own_plane = jnp.arange(count, dtype=jnp.int32) // ACTIVE + 1
    table_x = extended(volume, from_below[0], from_above[0])
    table_g = extended(grad_volume, from_below[1], from_above[1])
    padded = build_padded(volume, table_x, own_plane, own_cells, table_gid)
    grad_padded = build_padded(grad_volume, table_g, own_plane, own_cells, table_gid)
    w_flat = weight.reshape(TAPS * CHANNELS, CHANNELS)
    w_back = jnp.transpose(weight, (1, 0, 2)).reshape(CHANNELS, TAPS * CHANNELS)
    group = math.gcd(count, 4)
    group_count = count // group
    shape_p = (group_count, group, CHANNELS, EDGE + 2, EDGE + 2, EDGE + 2)
    mask_full = occupancy[0].astype(jnp.float32).reshape(group_count, group, VOXELS)

    def group_terms(inner):
        padded_p, grad_padded_p, mask_p, grad_masked_p = inner
        col_x = columns(padded_p, 1)
        col_g = columns(grad_padded_p, -1)
        result = jnp.einsum("kc,bkv->bcv", w_flat, col_x, preferred_element_type=jnp.float32)
        out_p = (result * mask_p[:, None, :]).astype(jnp.bfloat16)
        grad_w = jnp.einsum("bkv,bcv->kc", col_x, grad_masked_p, preferred_element_type=jnp.float32)
        back = jnp.einsum("ik,bkv->biv", w_back, col_g, preferred_element_type=jnp.float32)
        grad_p = (back * mask_p[:, None, :]).astype(jnp.bfloat16)
        return (out_p, grad_p, grad_w)

    outs_p, grads_p, weights_p = lax.map(
        group_terms,
        (
            padded.reshape(shape_p),
            grad_padded.reshape(shape_p),
            mask_full,
            grad_masked.reshape(group_count, group, CHANNELS, VOXELS),
        ),
    )
    local_grad = jnp.sum(weights_p, axis=0)
    grad_weight = lax.psum(local_grad, ("event", "blk"))
    grad_weight = grad_weight.reshape(TAPS, CHANNELS, CHANNELS)
    output = outs_p.reshape(count, CHANNELS, VOXELS)[None]
    grad_features = grads_p.reshape(count, CHANNELS, VOXELS)[None]
    return (output, grad_features, grad_weight)


def solution(mesh):
    in_specs = (
        P("event", "blk", None, None),
        P("event", "blk", None),
        P("event", None),
        P(),
        P("event", "blk", None, None),
    )
    out_specs = (P("event", "blk", None, None), P("event", "blk", None, None), P())
    return jax.shard_map(
        per_device, mesh=mesh, in_specs=in_specs, out_specs=out_specs, check_vma=False
    )
```

profile of v0, /device:TPU:0, one launch (start us, length us, event | category | flops | bytes accessed | tf_op | source)
XLA Modules:
  0.0 1134.5 jit_solution(11747880840834999203)
XLA Ops:
  9.0 4.1 copy.831
  13.1 2.8 copy.833
  15.9 4.3 broadcast_multiply_fusion.1
  21.4 4.2 copy.834
  25.7 2.7 copy.835
  28.3 3.1 collective-permute-start
  31.5 5.4 copy.838
  41.2 3.7 copy.879
  44.9 3.6 copy.829
  60.3 4.3 broadcast_multiply_fusion.2
  64.6 3.5 scatter.194
  68.2 3.6 scatter.241
  91.0 2.7 broadcast_multiply_fusion.4
  103.1 3.0 copy.841
  108.3 3.0 copy.881
  113.6 3.0 copy.883
  116.5 6.7 fusion.17
  180.6 2.6 copy.902
  214.1 2.6 copy.872
  216.7 2.6 copy.914
  251.1 2.6 fusion.31
  287.7 699.8 %while.72 = (s32[]{:T(128)}, bf16[6,4,64,512]{3,2,1,0:T(8,128)(2,1)}, bf16[6,4,64,512]{3,2,1,0:T(8,128)(2,1)}, f32[6,1728,64]{1,2,0:T(8,128)}, bf16[6,4,64,10,10...) while((s32[]{:T(128)}, ...), condition=%wide.region_53.61_spmd, body=%wide.region_52.60_spmd.sunk | while | flops 1359478784 | bytes 151677424 | solution.py:137
  307.4 4.0 fusion.204
  342.3 5.2 fusion.205
  362.4 3.9 fusion.201
  396.3 6.2 fusion.206
  424.0 4.0 fusion.204
  458.9 5.2 fusion.205
  479.0 3.9 fusion.201
  512.9 6.1 fusion.206
  540.6 4.0 fusion.204
  575.5 5.2 fusion.205
  595.6 3.9 fusion.201
  629.5 6.1 fusion.206
  657.2 4.0 fusion.204
  692.1 5.2 fusion.205
  712.2 3.9 fusion.201
  746.1 6.1 fusion.206
  773.8 4.0 fusion.204
  808.7 5.2 fusion.205
  828.8 3.9 fusion.201
  862.7 6.2 fusion.206
  890.4 4.0 fusion.204
  925.3 5.2 fusion.205
  945.4 3.9 fusion.201
  979.4 6.2 fusion.206
  991.0 133.9 %all-reduce.8.cloned.1.call-done = f32[27,64,64]{1,0,2:T(8,128)} async-done(((f32[27,64,64]{1,0,2:T(8,128)}), f32[27,64,64]{1,0,2:T(8,128)}) %all-reduce.8.cloned.1.call-update) | async-done | bytes 442384 | tf_op jit(solution)/shard_map/psum | solution.py:147
  1124.9 2.6 copy.923
  (1135 shorter events, 790.3 us)
Async XLA Ops:
  7.2 1117.7 %all-reduce.8.cloned.1.call-start = ((), (), s32[]{:S(2)}) async-start(), calls=%async_computation | async-start | bytes 2097152 | tf_op jit(solution)/shard_map/psum | solution.py:147
  21.4 19.5 %copy-start.54 = (s32[1,192]{1,0:T(1,128)S(1)}, s32[1,192]{1,0:T(1,128)}, u32[]{:S(2)}) copy-start(s32[1,192]{1,0:T(1,128)} %param.139) | copy-start | bytes 2308
  25.7 19.2 %copy-start.14 = (bf16[1,24,64,512]{3,2,1,0:T(8,128)(2,1)S(1)}, bf16[1,24,64,512]{3,2,1,0:T(8,128)(2,1)}, u32[]{:S(2)}) copy-start(bf16[1,24,64,512]{3,2,1,0:T(8,128)(2,1)} %param.137) | copy-start | bytes 4718596
  28.3 65.4 %collective-permute-start = (bf16[2,24,4096]{2,1,0:T(8,128)(2,1)}, bf16[2,24,4096]{2,1,0:T(8,128)(2,1)}, u32[]{:S(2)}, u32[]{:S(2)}) collective-permute-start(bf16[2,24,4096]{2,1,0:T(8,128)(2,1)} %copy.835), channel_id=1, source_target_pairs={{0,1},{1,2},{2,3},{3,4},{4,5},{5,6},{6,7},{8,9},{9,10},{10,11},{11... | collective-permute-start | bytes 1179656 | tf_op jit(solution)/shard_map/ppermute | solution.py:21
  39.4 59.7 %collective-permute-start.1 = (bf16[2,24,4096]{2,1,0:T(8,128)(2,1)}, bf16[2,24,4096]{2,1,0:T(8,128)(2,1)}, u32[]{:S(2)}, u32[]{:S(2)}) collective-permute-start(bf16[2,24,4096]{2,1,0:T(8,128)(2,1)} %copy.839), channel_id=1, source_target_pairs={{1,0},{2,1},{3,2},{4,3},{5,4},{6,5},{7,6},{9,8},{10,9},{11,10},{12... | collective-permute-start | bytes 1179656 | tf_op jit(solution)/shard_map/ppermute | solution.py:21
  91.0 151.1 %copy-start.53 = (s32[1024]{0:T(1024)}, s32[1024]{0:T(1024)S(1)}, u32[]{:S(2)}) copy-start(s32[1024]{0:T(1024)S(1)} %pad_clamp_fusion) | copy-start | bytes 12292
  244.8 24.9 %copy-start.24 = (bf16[24,64,8]{1,2,0:T(8,128)(2,1)S(1)}, bf16[24,64,8]{1,2,0:T(8,128)(2,1)}, u32[]{:S(2)}) copy-start(bf16[24,64,8]{1,2,0:T(8,128)(2,1)} %gather_fusion.14) | copy-start | bytes 73732
  244.9 24.9 %copy-start.25 = (bf16[24,64,8]{1,2,0:T(8,128)(2,1)S(1)}, bf16[24,64,8]{1,2,0:T(8,128)(2,1)}, u32[]{:S(2)}) copy-start(bf16[24,64,8]{1,2,0:T(8,128)(2,1)} %gather_fusion.40) | copy-start | bytes 73732
  244.9 28.4 %copy-start.26 = (bf16[24,64,8]{1,2,0:T(8,128)(2,1)S(1)}, bf16[24,64,8]{1,2,0:T(8,128)(2,1)}, u32[]{:S(2)}) copy-start(bf16[24,64,8]{1,2,0:T(8,128)(2,1)} %gather_fusion.16) | copy-start | bytes 73732
  244.9 28.4 %copy-start.27 = (bf16[24,64,8]{1,2,0:T(8,128)(2,1)S(1)}, bf16[24,64,8]{1,2,0:T(8,128)(2,1)}, u32[]{:S(2)}) copy-start(bf16[24,64,8]{1,2,0:T(8,128)(2,1)} %gather_fusion.42) | copy-start | bytes 73732
  244.9 29.9 %copy-start.51 = (bf16[24,64]{1,0:T(8,128)(2,1)S(1)}, bf16[24,64]{1,0:T(8,128)(2,1)}, u32[]{:S(2)}) copy-start(bf16[24,64]{1,0:T(8,128)(2,1)} %gather_fusion.17) | copy-start | bytes 9220
  244.9 29.9 %copy-start.52 = (bf16[24,64]{1,0:T(8,128)(2,1)S(1)}, bf16[24,64]{1,0:T(8,128)(2,1)}, u32[]{:S(2)}) copy-start(bf16[24,64]{1,0:T(8,128)(2,1)} %gather_fusion.43) | copy-start | bytes 9220
  244.9 31.2 %copy-start.22 = (bf16[24,64,8]{1,2,0:T(8,128)(2,1)S(1)}, bf16[24,64,8]{1,2,0:T(8,128)(2,1)}, u32[]{:S(2)}) copy-start(bf16[24,64,8]{1,2,0:T(8,128)(2,1)} %gather_fusion.18) | copy-start | bytes 73732
  244.9 31.2 %copy-start.23 = (bf16[24,64,8]{1,2,0:T(8,128)(2,1)S(1)}, bf16[24,64,8]{1,2,0:T(8,128)(2,1)}, u32[]{:S(2)}) copy-start(bf16[24,64,8]{1,2,0:T(8,128)(2,1)} %gather_fusion.44) | copy-start | bytes 73732
  244.9 32.6 %copy-start.49 = (bf16[24,64]{1,0:T(8,128)(2,1)S(1)}, bf16[24,64]{1,0:T(8,128)(2,1)}, u32[]{:S(2)}) copy-start(bf16[24,64]{1,0:T(8,128)(2,1)} %gather_fusion.19) | copy-start | bytes 9220
  244.9 32.6 %copy-start.50 = (bf16[24,64]{1,0:T(8,128)(2,1)S(1)}, bf16[24,64]{1,0:T(8,128)(2,1)}, u32[]{:S(2)}) copy-start(bf16[24,64]{1,0:T(8,128)(2,1)} %gather_fusion.45) | copy-start | bytes 9220
  244.9 33.9 %copy-start.18 = (bf16[24,64,8]{1,2,0:T(8,128)(2,1)S(1)}, bf16[24,64,8]{1,2,0:T(8,128)(2,1)}, u32[]{:S(2)}) copy-start(bf16[24,64,8]{1,2,0:T(8,128)(2,1)} %gather_fusion.20) | copy-start | bytes 73732
  245.0 33.9 %copy-start.19 = (bf16[24,64,8]{1,2,0:T(8,128)(2,1)S(1)}, bf16[24,64,8]{1,2,0:T(8,128)(2,1)}, u32[]{:S(2)}) copy-start(bf16[24,64,8]{1,2,0:T(8,128)(2,1)} %gather_fusion.46) | copy-start | bytes 73732
  245.0 37.4 %copy-start.20 = (bf16[24,64,8]{1,2,0:T(8,128)(2,1)S(1)}, bf16[24,64,8]{1,2,0:T(8,128)(2,1)}, u32[]{:S(2)}) copy-start(bf16[24,64,8]{1,2,0:T(8,128)(2,1)} %gather_fusion.48) | copy-start | bytes 73732
  245.0 37.4 %copy-start.21 = (bf16[24,64,8]{1,2,0:T(8,128)(2,1)S(1)}, bf16[24,64,8]{1,2,0:T(8,128)(2,1)}, u32[]{:S(2)}) copy-start(bf16[24,64,8]{1,2,0:T(8,128)(2,1)} %gather_fusion.22) | copy-start | bytes 73732
  245.0 38.8 %copy-start.47 = (bf16[24,64]{1,0:T(8,128)(2,1)S(1)}, bf16[24,64]{1,0:T(8,128)(2,1)}, u32[]{:S(2)}) copy-start(bf16[24,64]{1,0:T(8,128)(2,1)} %gather_fusion.49) | copy-start | bytes 9220
  245.0 38.7 %copy-start.48 = (bf16[24,64]{1,0:T(8,128)(2,1)S(1)}, bf16[24,64]{1,0:T(8,128)(2,1)}, u32[]{:S(2)}) copy-start(bf16[24,64]{1,0:T(8,128)(2,1)} %gather_fusion.23) | copy-start | bytes 9220
  245.0 40.1 %copy-start.16 = (bf16[24,64,8]{1,2,0:T(8,128)(2,1)S(1)}, bf16[24,64,8]{1,2,0:T(8,128)(2,1)}, u32[]{:S(2)}) copy-start(bf16[24,64,8]{1,2,0:T(8,128)(2,1)} %gather_fusion.50) | copy-start | bytes 73732
  245.0 40.1 %copy-start.17 = (bf16[24,64,8]{1,2,0:T(8,128)(2,1)S(1)}, bf16[24,64,8]{1,2,0:T(8,128)(2,1)}, u32[]{:S(2)}) copy-start(bf16[24,64,8]{1,2,0:T(8,128)(2,1)} %gather_fusion.24) | copy-start | bytes 73732
  321.5 16.3 %copy-start.3 = (bf16[4,64,8,8,8]{1,4,3,2,0:T(8,128)(2,1)S(1)}, bf16[4,64,8,8,8]{1,4,3,2,0:T(8,128)(2,1)}, u32[]{:S(2)}) copy-start(bf16[4,64,8,8,8]{1,4,3,2,0:T(8,128)(2,1)} %get-tuple-element.1383) | copy-start | bytes 786436 | tf_op jit(solution)/shard_map/while
  322.5 16.3 %copy-start.2 = (bf16[4,64,8,8,8]{1,4,3,2,0:T(8,128)(2,1)S(1)}, bf16[4,64,8,8,8]{1,4,3,2,0:T(8,128)(2,1)}, u32[]{:S(2)}) copy-start(bf16[4,64,8,8,8]{1,4,3,2,0:T(8,128)(2,1)} %get-tuple-element.1384) | copy-start | bytes 786436 | tf_op jit(solution)/shard_map/while
  323.4 16.3 %copy-start.1 = (bf16[4,64,8,8,8]{1,4,3,2,0:T(8,128)(2,1)S(1)}, bf16[4,64,8,8,8]{1,4,3,2,0:T(8,128)(2,1)}, u32[]{:S(2)}) copy-start(bf16[4,64,8,8,8]{1,4,3,2,0:T(8,128)(2,1)} %get-tuple-element.1385) | copy-start | bytes 786436 | tf_op jit(solution)/shard_map/while
  373.4 17.3 %copy-start.6 = (bf16[4,64,8,8,8]{1,4,3,2,0:T(8,128)(2,1)S(1)}, bf16[4,64,8,8,8]{1,4,3,2,0:T(8,128)(2,1)}, u32[]{:S(2)}) copy-start(bf16[4,64,8,8,8]{1,4,3,2,0:T(8,128)(2,1)} %get-tuple-element.1353) | copy-start | bytes 786436 | tf_op jit(solution)/shard_map/while
  438.1 16.3 %copy-start.3 = (bf16[4,64,8,8,8]{1,4,3,2,0:T(8,128)(2,1)S(1)}, bf16[4,64,8,8,8]{1,4,3,2,0:T(8,128)(2,1)}, u32[]{:S(2)}) copy-start(bf16[4,64,8,8,8]{1,4,3,2,0:T(8,128)(2,1)} %get-tuple-element.1383) | copy-start | bytes 786436 | tf_op jit(solution)/shard_map/while
  439.1 16.3 %copy-start.2 = (bf16[4,64,8,8,8]{1,4,3,2,0:T(8,128)(2,1)S(1)}, bf16[4,64,8,8,8]{1,4,3,2,0:T(8,128)(2,1)}, u32[]{:S(2)}) copy-start(bf16[4,64,8,8,8]{1,4,3,2,0:T(8,128)(2,1)} %get-tuple-element.1384) | copy-start | bytes 786436 | tf_op jit(solution)/shard_map/while
  440.0 16.3 %copy-start.1 = (bf16[4,64,8,8,8]{1,4,3,2,0:T(8,128)(2,1)S(1)}, bf16[4,64,8,8,8]{1,4,3,2,0:T(8,128)(2,1)}, u32[]{:S(2)}) copy-start(bf16[4,64,8,8,8]{1,4,3,2,0:T(8,128)(2,1)} %get-tuple-element.1385) | copy-start | bytes 786436 | tf_op jit(solution)/shard_map/while
  490.0 17.3 %copy-start.6 = (bf16[4,64,8,8,8]{1,4,3,2,0:T(8,128)(2,1)S(1)}, bf16[4,64,8,8,8]{1,4,3,2,0:T(8,128)(2,1)}, u32[]{:S(2)}) copy-start(bf16[4,64,8,8,8]{1,4,3,2,0:T(8,128)(2,1)} %get-tuple-element.1353) | copy-start | bytes 786436 | tf_op jit(solution)/shard_map/while
  554.7 16.3 %copy-start.3 = (bf16[4,64,8,8,8]{1,4,3,2,0:T(8,128)(2,1)S(1)}, bf16[4,64,8,8,8]{1,4,3,2,0:T(8,128)(2,1)}, u32[]{:S(2)}) copy-start(bf16[4,64,8,8,8]{1,4,3,2,0:T(8,128)(2,1)} %get-tuple-element.1383) | copy-start | bytes 786436 | tf_op jit(solution)/shard_map/while
  555.7 16.3 %copy-start.2 = (bf16[4,64,8,8,8]{1,4,3,2,0:T(8,128)(2,1)S(1)}, bf16[4,64,8,8,8]{1,4,3,2,0:T(8,128)(2,1)}, u32[]{:S(2)}) copy-start(bf16[4,64,8,8,8]{1,4,3,2,0:T(8,128)(2,1)} %get-tuple-element.1384) | copy-start | bytes 786436 | tf_op jit(solution)/shard_map/while
  556.6 16.3 %copy-start.1 = (bf16[4,64,8,8,8]{1,4,3,2,0:T(8,128)(2,1)S(1)}, bf16[4,64,8,8,8]{1,4,3,2,0:T(8,128)(2,1)}, u32[]{:S(2)}) copy-start(bf16[4,64,8,8,8]{1,4,3,2,0:T(8,128)(2,1)} %get-tuple-element.1385) | copy-start | bytes 786436 | tf_op jit(solution)/shard_map/while
  606.6 17.3 %copy-start.6 = (bf16[4,64,8,8,8]{1,4,3,2,0:T(8,128)(2,1)S(1)}, bf16[4,64,8,8,8]{1,4,3,2,0:T(8,128)(2,1)}, u32[]{:S(2)}) copy-start(bf16[4,64,8,8,8]{1,4,3,2,0:T(8,128)(2,1)} %get-tuple-element.1353) | copy-start | bytes 786436 | tf_op jit(solution)/shard_map/while
  671.3 16.3 %copy-start.3 = (bf16[4,64,8,8,8]{1,4,3,2,0:T(8,128)(2,1)S(1)}, bf16[4,64,8,8,8]{1,4,3,2,0:T(8,128)(2,1)}, u32[]{:S(2)}) copy-start(bf16[4,64,8,8,8]{1,4,3,2,0:T(8,128)(2,1)} %get-tuple-element.1383) | copy-start | bytes 786436 | tf_op jit(solution)/shard_map/while
  672.3 16.3 %copy-start.2 = (bf16[4,64,8,8,8]{1,4,3,2,0:T(8,128)(2,1)S(1)}, bf16[4,64,8,8,8]{1,4,3,2,0:T(8,128)(2,1)}, u32[]{:S(2)}) copy-start(bf16[4,64,8,8,8]{1,4,3,2,0:T(8,128)(2,1)} %get-tuple-element.1384) | copy-start | bytes 786436 | tf_op jit(solution)/shard_map/while
  673.2 16.3 %copy-start.1 = (bf16[4,64,8,8,8]{1,4,3,2,0:T(8,128)(2,1)S(1)}, bf16[4,64,8,8,8]{1,4,3,2,0:T(8,128)(2,1)}, u32[]{:S(2)}) copy-start(bf16[4,64,8,8,8]{1,4,3,2,0:T(8,128)(2,1)} %get-tuple-element.1385) | copy-start | bytes 786436 | tf_op jit(solution)/shard_map/while
  723.2 17.3 %copy-start.6 = (bf16[4,64,8,8,8]{1,4,3,2,0:T(8,128)(2,1)S(1)}, bf16[4,64,8,8,8]{1,4,3,2,0:T(8,128)(2,1)}, u32[]{:S(2)}) copy-start(bf16[4,64,8,8,8]{1,4,3,2,0:T(8,128)(2,1)} %get-tuple-element.1353) | copy-start | bytes 786436 | tf_op jit(solution)/shard_map/while
  787.9 16.3 %copy-start.3 = (bf16[4,64,8,8,8]{1,4,3,2,0:T(8,128)(2,1)S(1)}, bf16[4,64,8,8,8]{1,4,3,2,0:T(8,128)(2,1)}, u32[]{:S(2)}) copy-start(bf16[4,64,8,8,8]{1,4,3,2,0:T(8,128)(2,1)} %get-tuple-element.1383) | copy-start | bytes 786436 | tf_op jit(solution)/shard_map/while
  788.9 16.3 %copy-start.2 = (bf16[4,64,8,8,8]{1,4,3,2,0:T(8,128)(2,1)S(1)}, bf16[4,64,8,8,8]{1,4,3,2,0:T(8,128)(2,1)}, u32[]{:S(2)}) copy-start(bf16[4,64,8,8,8]{1,4,3,2,0:T(8,128)(2,1)} %get-tuple-element.1384) | copy-start | bytes 786436 | tf_op jit(solution)/shard_map/while
  789.8 16.3 %copy-start.1 = (bf16[4,64,8,8,8]{1,4,3,2,0:T(8,128)(2,1)S(1)}, bf16[4,64,8,8,8]{1,4,3,2,0:T(8,128)(2,1)}, u32[]{:S(2)}) copy-start(bf16[4,64,8,8,8]{1,4,3,2,0:T(8,128)(2,1)} %get-tuple-element.1385) | copy-start | bytes 786436 | tf_op jit(solution)/shard_map/while
  839.8 17.3 %copy-start.6 = (bf16[4,64,8,8,8]{1,4,3,2,0:T(8,128)(2,1)S(1)}, bf16[4,64,8,8,8]{1,4,3,2,0:T(8,128)(2,1)}, u32[]{:S(2)}) copy-start(bf16[4,64,8,8,8]{1,4,3,2,0:T(8,128)(2,1)} %get-tuple-element.1353) | copy-start | bytes 786436 | tf_op jit(solution)/shard_map/while
  904.6 16.3 %copy-start.3 = (bf16[4,64,8,8,8]{1,4,3,2,0:T(8,128)(2,1)S(1)}, bf16[4,64,8,8,8]{1,4,3,2,0:T(8,128)(2,1)}, u32[]{:S(2)}) copy-start(bf16[4,64,8,8,8]{1,4,3,2,0:T(8,128)(2,1)} %get-tuple-element.1383) | copy-start | bytes 786436 | tf_op jit(solution)/shard_map/while
  905.5 16.3 %copy-start.2 = (bf16[4,64,8,8,8]{1,4,3,2,0:T(8,128)(2,1)S(1)}, bf16[4,64,8,8,8]{1,4,3,2,0:T(8,128)(2,1)}, u32[]{:S(2)}) copy-start(bf16[4,64,8,8,8]{1,4,3,2,0:T(8,128)(2,1)} %get-tuple-element.1384) | copy-start | bytes 786436 | tf_op jit(solution)/shard_map/while
  906.4 16.3 %copy-start.1 = (bf16[4,64,8,8,8]{1,4,3,2,0:T(8,128)(2,1)S(1)}, bf16[4,64,8,8,8]{1,4,3,2,0:T(8,128)(2,1)}, u32[]{:S(2)}) copy-start(bf16[4,64,8,8,8]{1,4,3,2,0:T(8,128)(2,1)} %get-tuple-element.1385) | copy-start | bytes 786436 | tf_op jit(solution)/shard_map/while
  956.5 17.3 %copy-start.6 = (bf16[4,64,8,8,8]{1,4,3,2,0:T(8,128)(2,1)S(1)}, bf16[4,64,8,8,8]{1,4,3,2,0:T(8,128)(2,1)}, u32[]{:S(2)}) copy-start(bf16[4,64,8,8,8]{1,4,3,2,0:T(8,128)(2,1)} %get-tuple-element.1353) | copy-start | bytes 786436 | tf_op jit(solution)/shard_map/while
  (70 other events, 707.6 us)
Sparse Core Ops, SparseCore 0:
  991.1 133.7 all-reduce.7
where the time goes:
time: 1150 us; the launch traced here: 1130 us
  local copies, waits for them, and re-layouts  808 us (70%)
  waiting for transfers between devices  134 us (12%)
  other arithmetic  89.4 us (8%)
  matrix products  80.3 us (7%)
  between operations  15 us (1%)
    reshape x324, local copies, waits for them, and re-layouts, columns(): pieces.append(piece.reshape(padded.shape[0], CHANNELS, VOXELS))  287 us
    while x456, local copies, waits for them, and re-layouts  226 us
    psum x1, waiting for transfers between devices, per_device(): grad_weight = lax.psum(local_grad, ('event', 'blk'))  134 us
    gather x52, local copies, waits for them, and re-layouts, build_padded(): picked = jnp.take(slab, position, axis=0)  76.1 us
    slice x24, local copies, waits for them, and re-layouts, columns(): padded[:, :, starts[0]:starts[0] + EDGE, starts[1]:starts[1] + EDGE, star...  73.4 us
    another operation x50, local copies, waits for them, and re-layouts, build_padded(): picked = jnp.take(slab, position, axis=0)  44.9 us
    scatter x26, other arithmetic, build_padded(): padded = padded.at[:, :, dest_x, dest_y, dest_z].set(picked)  42.7 us
    dot_general x6, matrix products, group_terms(): jnp.einsum('bkv,bcv->kc', col_x, grad_masked_p, preferred_element_type=jn...  36.9 us
  transfers between devices with their start and end apart: 3, of which 1 were waited for; matrix products, arithmetic and copies ran while one was open for 6% of the time, Pallas kernels for 0%

commit v1 on v0

v1 whole, which is shorter than its diff:
```python
import functools

import jax
import jax.numpy as jnp
from jax import lax
from jax.experimental import pallas as pl
from jax.experimental.pallas import tpu as pltpu
from jax.sharding import PartitionSpec as P

CHANNELS = 64
EDGE = 8
VOXELS = 512
FACE = EDGE * EDGE
TAPS = 27
GRID_Y = 8
GRID_Z = 8
ACTIVE = 24
PAIR = 2 * CHANNELS
HALF = TAPS // 2 + 1


def shifted(x, axis, by):
    devices = lax.axis_size(axis)
    pairs = [(i, i + by) for i in range(devices) if 0 <= i + by < devices]
    return lax.ppermute(x, axis, pairs)


def place(cell):
    return cell // GRID_Z * EDGE, pl.multiple_of(cell % GRID_Z * EDGE, EDGE)


def kernel(do_conv, do_gw, cells, x_ref, g_ref, occ_ref, lo_ref, hi_ref, *rest):
    rest = list(rest)
    w_ref = rest.pop(0) if do_conv else None
    out_ref, back_ref = (rest.pop(0), rest.pop(0)) if do_conv else (None, None)
    gw_ref = rest.pop(0) if do_gw else None
    plane, cols = rest[0], rest[1]
    rows_ref = rest[2] if do_gw else None

    def clear(i, _):
        plane[i] = jnp.zeros(plane.shape[1:], plane.dtype)
        return 0

    lax.fori_loop(0, EDGE + 2, clear, 0)
    if do_gw:
        gw_ref[...] = jnp.zeros(gw_ref.shape, gw_ref.dtype)

    def scatter(b, _):
        mask = occ_ref[pl.ds(b, 1), :].astype(jnp.float32)
        both = jnp.concatenate(
            [x_ref[b].astype(jnp.float32) * mask, g_ref[b].astype(jnp.float32) * mask], axis=0
        )
        if do_gw:
            rows_ref[b] = both.astype(jnp.bfloat16)
        y, z = place(cells[1, b])
        plane[1 : EDGE + 1, pl.ds(y + 1, EDGE), pl.ds(z + EDGE, EDGE), :] = both.T.reshape(
            EDGE, EDGE, EDGE, PAIR
        )
        y, z = place(cells[0, b])
        plane[0, pl.ds(y + 1, EDGE), pl.ds(z + EDGE, EDGE), :] = (
            lo_ref[b].astype(jnp.float32).reshape(EDGE, EDGE, PAIR)
        )
        y, z = place(cells[2, b])
        plane[EDGE + 1, pl.ds(y + 1, EDGE), pl.ds(z + EDGE, EDGE), :] = (
            hi_ref[b].astype(jnp.float32).reshape(EDGE, EDGE, PAIR)
        )
        return 0

    lax.fori_loop(0, ACTIVE, scatter, 0)

    def block(b, _):
        y, z = place(cells[1, b])
        for c in range(3):
            for e in range(3):
                part = plane[:, pl.ds(y + c, EDGE), pl.ds(z + EDGE - 1 + e, EDGE), :]
                at = (3 * c + e) * PAIR
                cols[:, at : at + PAIR] = part.reshape((EDGE + 2) * FACE, PAIR).astype(jnp.bfloat16)
        if do_gw:
            rows = rows_ref[b]
            gw_ref[:, : 5 * PAIR] += jnp.dot(
                rows, cols[FACE : FACE + VOXELS, 4 * PAIR :], preferred_element_type=jnp.float32
            )
            gw_ref[:, 5 * PAIR :] += jnp.dot(
                rows, cols[2 * FACE :, :], preferred_element_type=jnp.float32
            )
        if do_conv:
            total = jnp.dot(cols[:VOXELS, :], w_ref[0], preferred_element_type=jnp.float32)
            for a in (1, 2):
                total += jnp.dot(
                    cols[a * FACE : a * FACE + VOXELS, :],
                    w_ref[a],
                    preferred_element_type=jnp.float32,
                )
            mask = occ_ref[pl.ds(b, 1), :].astype(jnp.float32)
            result = (total.T * mask).astype(jnp.bfloat16)
            out_ref[b] = result[:CHANNELS]
            back_ref[b] = result[CHANNELS:]
        return 0

    lax.fori_loop(0, ACTIVE, block, 0)


def run(do_conv, do_gw, cells, x, g, occ, lo, hi, w):
    vmem = pl.BlockSpec(memory_space=pltpu.VMEM)
    operands = [cells, x, g, occ, lo, hi]
    shapes = []
    scratch = [
        pltpu.VMEM((EDGE + 2, GRID_Y * EDGE + 2, (GRID_Z + 2) * EDGE, PAIR), jnp.float32),
        pltpu.VMEM(((EDGE + 2) * FACE, 9 * PAIR), jnp.bfloat16),
    ]
    flops = 0
    if do_conv:
        operands.append(w)
        shapes += [jax.ShapeDtypeStruct(x.shape, x.dtype)] * 2
        flops += 4 * ACTIVE * VOXELS * TAPS * CHANNELS * PAIR * 2
    if do_gw:
        shapes.append(jax.ShapeDtypeStruct((PAIR, HALF * PAIR), jnp.float32))
        scratch.append(pltpu.VMEM((ACTIVE, PAIR, VOXELS), jnp.bfloat16))
        flops += 2 * ACTIVE * VOXELS * HALF * PAIR * PAIR * 2
    return pl.pallas_call(
        functools.partial(kernel, do_conv, do_gw),
        out_shape=shapes,
        in_specs=[pl.BlockSpec(memory_space=pltpu.SMEM)] + [vmem] * (len(operands) - 1),
        out_specs=[vmem] * len(shapes),
        scratch_shapes=scratch,
        cost_estimate=pl.CostEstimate(flops=flops, bytes_accessed=8 * x.size, transcendentals=0),
        compiler_params=pltpu.CompilerParams(vmem_limit_bytes=56 * 1024 * 1024),
    )(*operands)


def per_device(features, occupancy, block_cells, weight, cotangent):
    device = lax.axis_index("blk")
    x, g, occ = features[0], cotangent[0], occupancy[0]
    half = occ.astype(jnp.bfloat16)

    def faces(at):
        part = jnp.concatenate([x[:, :, at : at + FACE], g[:, :, at : at + FACE]], axis=1)
        part = part * half[:, None, at : at + FACE]
        return jnp.transpose(part, (0, 2, 1))

    from_below = shifted(faces(VOXELS - FACE), "blk", 1)
    from_above = shifted(faces(0), "blk", -1)
    filler = block_cells[0, :ACTIVE]
    listed = jnp.concatenate([filler, block_cells[0], filler])
    cells = lax.dynamic_slice_in_dim(listed, device * ACTIVE, 3 * ACTIVE).reshape(3, ACTIVE)
    none = jnp.zeros_like(weight)
    turned = jnp.transpose(weight[::-1], (0, 2, 1))
    w = jnp.concatenate(
        [jnp.concatenate([weight, none], axis=2), jnp.concatenate([none, turned], axis=2)], axis=1
    ).reshape(3, 9 * PAIR, PAIR)
    if SPLIT:
        (terms,) = run(False, True, cells, x, g, occ, from_below, from_above, w)
    else:
        output, back, terms = run(True, True, cells, x, g, occ, from_below, from_above, w)
    terms = terms.reshape(PAIR, HALF, PAIR)
    upper = jnp.transpose(terms[CHANNELS:, :, :CHANNELS], (1, 2, 0))
    lower = jnp.transpose(terms[:CHANNELS, :0:-1, CHANNELS:], (1, 0, 2))
    local = jnp.concatenate([lower, upper], axis=0).reshape(-1, PAIR)
    grad_weight = lax.psum(local, ("event", "blk")).reshape(TAPS, CHANNELS, CHANNELS)
    if SPLIT:
        output, back = run(True, False, cells, x, g, occ, from_below, from_above, w)
    return (output[None], back[None], grad_weight)


SPLIT = False


def solution(mesh):
    in_specs = (
        P("event", "blk", None, None),
        P("event", "blk", None),
        P("event", None),
        P(),
        P("event", "blk", None, None),
    )
    out_specs = (P("event", "blk", None, None), P("event", "blk", None, None), P())
    return jax.shard_map(
        per_device, mesh=mesh, in_specs=in_specs, out_specs=out_specs, check_vma=False
    )
```

time: 1150 us -> 222 us (0.19); the launches traced: 1130 us -> 221 us
  local copies, waits for them, and re-layouts: 808 us -> 16.1 us
  other arithmetic: 89.4 us -> 2.17 us
  matrix products: 80.3 us -> 0 us
  Pallas kernels: 0 us -> 47.7 us
    reshape x327 -> x1, local copies, waits for them, and re-layouts: 293 us -> 0.65 us  [per_device(): lax.dynamic_slice_in_dim(listed, device * ACTIVE, 3 * ACTIVE)]
    while x456 -> x0, local copies, waits for them, and re-layouts: 226 us -> none
    slice x32 -> x3, local copies, waits for them, and re-layouts: 94.7 us -> 1.35 us  [the longest x1 1.25 us: faces(): x[:, :, at:at + FACE]]
    dot_general x18 -> x0, matrix products: 80.3 us -> none  [the longest x6 36.9 us: group_terms(): jnp.einsum('bkv,bcv->kc', col_x, grad_masked_p, preferred_element_type=jn...]
    gather x52 -> x0, local copies, waits for them, and re-layouts: 76.1 us -> none  [build_padded(): picked = jnp.take(slab, position, axis=0)]
    another operation x57 -> x0, local copies, waits for them, and re-layouts: 61.3 us -> none  [the longest x50 44.9 us: build_padded(): picked = jnp.take(slab, position, axis=0)]
    pallas_call x0 -> x1, Pallas kernels: none -> 47.7 us  [run(): pl.pallas_call(functools.partial(kernel, do_conv, do_gw), out_shape=shape...]
    scatter x26 -> x0, other arithmetic: 42.7 us -> none  [build_padded(): padded = padded.at[:, :, dest_x, dest_y, dest_z].set(picked)]
  transfers between devices with their start and end apart: 3 -> 3, of which waited for: 1 -> 1; matrix products, arithmetic and copies ran while one was open for 6% -> 2% of each run, Pallas kernels for 0% -> 0%
where the time goes in v1:
time: 222 us; the launch traced here: 221 us
  waiting for transfers between devices  137 us (62%)
  Pallas kernels  47.7 us (21%)
  local copies, waits for them, and re-layouts  16.1 us (7%)
  between operations  14.2 us (6%)
  starting transfers between devices  4.38 us (2%)
    psum x1, waiting for transfers between devices, per_device(): lax.psum(local, ('event', 'blk')).reshape(TAPS, CHANNELS, CHANNELS)  137 us
    pallas_call x1, Pallas kernels, run(): pl.pallas_call(functools.partial(kernel, do_conv, do_gw), out_shape=shape...  47.7 us
    unnamed x15, local copies, waits for them, and re-layouts  10.7 us
  transfers between devices with their start and end apart: 3, of which 1 were waited for; matrix products, arithmetic and copies ran while one was open for 2% of the time, Pallas kernels for 0%

profile of v1, /device:TPU:0, one launch (start us, length us, event | category | flops | bytes accessed | tf_op | source)
XLA Modules:
  0.0 221.5 jit_solution(3248919879546432094)
XLA Ops:
  7.2 0.0 all-reduce.4.cloned.1.call-start
  7.2 3.1 %copy.16 = bf16[1,24,64,512]{2,3,1,0:T(8,128)(2,1)S(1)} copy(bf16[1,24,64,512]{3,2,1,0:T(8,128)(2,1)} %param.5) | data formatting | bytes 3145728 | tf_op args[0]
  10.3 0.0 copy-start.1
  10.3 4.1 %copy.17 = bf16[1,24,64,512]{2,3,1,0:T(8,128)(2,1)} copy(bf16[1,24,64,512]{3,2,1,0:T(8,128)(2,1)} %param.9) | data formatting | bytes 3145728 | tf_op args[4]
  14.4 0.0 copy-done.1
  14.4 0.1 fusion.7
  14.5 1.2 fusion.5
  15.8 0.0 copy-start.2
  15.8 0.0 copy-start
  15.8 0.4 fusion.4
  16.2 1.3 collective-permute-start.1
  17.5 0.4 fusion.3
  17.9 3.1 %collective-permute-start = (bf16[24,64,128]{2,1,0:T(8,128)(2,1)S(1)}, bf16[24,64,128]{2,1,0:T(8,128)(2,1)S(1)}, u32[]{:S(2)}, u32[]{:S(2)}) collective-permute-start(bf16[24,64,128]{2,1,0:T(8,128)(2,1)S(1)} %fusion.3), channel_id=1, source_target_pairs={{0,1},{1,2},{2,3},{3,4},{4,5},{5,6},{6,7},{8,9},{9,10},{10,11},{11... | collective-permute-start | bytes 1179656 | tf_op jit(solution)/shard_map/ppermute | solution.py:25
  20.9 0.0 copy-done.2
  20.9 0.1 pad_add_fusion
  21.0 0.1 dynamic_slice.3
  21.1 0.7 reshape.23.cells
  21.7 0.0 copy-done
  21.8 0.2 copy.18
  22.0 0.4 fusion.2
  22.4 1.6 copy.19
  24.1 0.0 collective-permute-done.1.hi_ref
  24.1 0.0 copy-start.3
  24.1 0.0 collective-permute-done.lo_ref
  24.1 0.0 copy-start.4
  24.1 0.7 copy-done.3
  24.8 0.1 copy-done.4
  24.9 47.7 %shard_map.76 = (bf16[24,64,512]{2,1,0:T(8,128)(2,1)}, bf16[24,64,512]{2,1,0:T(8,128)(2,1)}, f32[128,1792]{1,0:T(8,128)}) custom-call(s32[3,24]{1,0:T(4,128)} %reshape.23.cells, bf16[24,64,512]{2,1,0:T(8,128)(2,1)} %bitcast.27, bf16[24,64,512]{2,1,0:T(8,128)(2,1)} %bitcast.28, s32[24,512]{1,0:T(8,128)} %bitcast.30, bf16[24,64,128]{2,1,0:T(8,128)(2,1)} %copy-done.4, ...), custom_call_target="tpu_custom_call" | custom-call | flops 33017561088 | bytes 6291456 | tf_op jit(solution)/shard_map/pallas_call | solution.py:120
  72.7 1.5 copy.22
  74.2 0.2 slice_bitcast_fusion
  74.4 0.2 copy.26
  74.6 1.0 pad_maximum_fusion
  75.6 0.0 all-reduce.4.cloned.1.call-update
  75.6 136.9 %all-reduce.4.cloned.1.call-done = f32[27,64,64]{2,1,0:T(8,128)} async-done(((f32[27,64,64]{2,1,0:T(8,128)}), f32[27,64,64]{2,1,0:T(8,128)}) %all-reduce.4.cloned.1.call-update) | async-done | bytes 442384 | tf_op jit(solution)/shard_map/psum | solution.py:159
  212.5 2.2 copy.28
  (5 shorter events, 0.1 us)
Async XLA Ops:
  7.2 205.3 %all-reduce.4.cloned.1.call-start = ((), (), s32[]{:S(2)}) async-start(), calls=%async_computation | async-start | bytes 1769472 | tf_op jit(solution)/shard_map/psum | solution.py:159
  10.3 4.1 %copy-start.1 = (s32[1,24,512]{2,1,0:T(8,128)S(1)}, s32[1,24,512]{2,1,0:T(8,128)}, u32[]{:S(2)}) copy-start(s32[1,24,512]{2,1,0:T(8,128)} %param.6) | copy-start | bytes 147460
  15.8 5.2 %copy-start.2 = (s32[1,192]{1,0:T(1,128)S(1)}, s32[1,192]{1,0:T(1,128)}, u32[]{:S(2)}) copy-start(s32[1,192]{1,0:T(1,128)} %param.7) | copy-start | bytes 2308
  15.8 6.0 %copy-start = (bf16[27,64,64]{2,1,0:T(8,128)(2,1)S(1)}, bf16[27,64,64]{2,1,0:T(8,128)(2,1)}, u32[]{:S(2)}) copy-start(bf16[27,64,64]{2,1,0:T(8,128)(2,1)} %param.8) | copy-start | bytes 663556
  16.2 7.9 %collective-permute-start.1 = (bf16[24,64,128]{2,1,0:T(8,128)(2,1)S(1)}, bf16[24,64,128]{2,1,0:T(8,128)(2,1)S(1)}, u32[]{:S(2)}, u32[]{:S(2)}) collective-permute-start(bf16[24,64,128]{2,1,0:T(8,128)(2,1)S(1)} %fusion.4), channel_id=1, source_target_pairs={{1,0},{2,1},{3,2},{4,3},{5,4},{6,5},{7,6},{9,8},{10,9},{11,10},{12... | collective-permute-start | bytes 1179656 | tf_op jit(solution)/shard_map/ppermute | solution.py:25
  17.9 6.2 %collective-permute-start = (bf16[24,64,128]{2,1,0:T(8,128)(2,1)S(1)}, bf16[24,64,128]{2,1,0:T(8,128)(2,1)S(1)}, u32[]{:S(2)}, u32[]{:S(2)}) collective-permute-start(bf16[24,64,128]{2,1,0:T(8,128)(2,1)S(1)} %fusion.3), channel_id=1, source_target_pairs={{0,1},{1,2},{2,3},{3,4},{4,5},{5,6},{6,7},{8,9},{9,10},{10,11},{11... | collective-permute-start | bytes 1179656 | tf_op jit(solution)/shard_map/ppermute | solution.py:25
  24.1 0.7 copy-start.3
  24.1 0.9 copy-start.4
Sparse Core Ops, SparseCore 0:
  75.7 136.6 all-reduce.3

commit v2 on v1

--- a/solution.py
+++ b/solution.py
@@ -29,6 +29,11 @@
     return cell // GRID_Z * EDGE, pl.multiple_of(cell % GRID_Z * EDGE, EDGE)
 
 
+def turned(face):
+    face = face.astype(jnp.float32)
+    return jnp.concatenate([face[:, :FACE], face[:, FACE:]], axis=0).T
+
+
 def kernel(do_conv, do_gw, cells, x_ref, g_ref, occ_ref, lo_ref, hi_ref, *rest):
     rest = list(rest)
     w_ref = rest.pop(0) if do_conv else None
@@ -42,8 +47,20 @@
         return 0
 
     lax.fori_loop(0, EDGE + 2, clear, 0)
+    if do_conv:
+        taps_ref = rest[-1]
+        none = jnp.zeros((CHANNELS, CHANNELS), jnp.float32)
+        for t in range(TAPS):
+            a, at = t // 9, t % 9 * PAIR
+            ahead = w_ref[t].astype(jnp.float32)
+            behind = w_ref[TAPS - 1 - t].astype(jnp.float32).T
+            taps_ref[a, at : at + CHANNELS] = jnp.concatenate([ahead, none], axis=1).astype(jnp.bfloat16)
+            taps_ref[a, at + CHANNELS : at + PAIR] = jnp.concatenate([none, behind], axis=1).astype(
+                jnp.bfloat16
+            )
     if do_gw:
-        gw_ref[...] = jnp.zeros(gw_ref.shape, gw_ref.dtype)
+        sums = rest[3]
+        sums[...] = jnp.zeros(sums.shape, sums.dtype)
 
     def scatter(b, _):
         mask = occ_ref[pl.ds(b, 1), :].astype(jnp.float32)
@@ -58,11 +75,11 @@
         )
         y, z = place(cells[0, b])
         plane[0, pl.ds(y + 1, EDGE), pl.ds(z + EDGE, EDGE), :] = (
-            lo_ref[b].astype(jnp.float32).reshape(EDGE, EDGE, PAIR)
+            turned(lo_ref[b]).reshape(EDGE, EDGE, PAIR)
         )
         y, z = place(cells[2, b])
         plane[EDGE + 1, pl.ds(y + 1, EDGE), pl.ds(z + EDGE, EDGE), :] = (
-            hi_ref[b].astype(jnp.float32).reshape(EDGE, EDGE, PAIR)
+            turned(hi_ref[b]).reshape(EDGE, EDGE, PAIR)
         )
         return 0
 
@@ -77,18 +94,18 @@
                 cols[:, at : at + PAIR] = part.reshape((EDGE + 2) * FACE, PAIR).astype(jnp.bfloat16)
         if do_gw:
             rows = rows_ref[b]
-            gw_ref[:, : 5 * PAIR] += jnp.dot(
+            sums[:, : 5 * PAIR] += jnp.dot(
                 rows, cols[FACE : FACE + VOXELS, 4 * PAIR :], preferred_element_type=jnp.float32
             )
-            gw_ref[:, 5 * PAIR :] += jnp.dot(
+            sums[:, 5 * PAIR :] += jnp.dot(
                 rows, cols[2 * FACE :, :], preferred_element_type=jnp.float32
             )
         if do_conv:
-            total = jnp.dot(cols[:VOXELS, :], w_ref[0], preferred_element_type=jnp.float32)
+            total = jnp.dot(cols[:VOXELS, :], taps_ref[0], preferred_element_type=jnp.float32)
             for a in (1, 2):
                 total += jnp.dot(
                     cols[a * FACE : a * FACE + VOXELS, :],
-                    w_ref[a],
+                    taps_ref[a],
                     preferred_element_type=jnp.float32,
                 )
             mask = occ_ref[pl.ds(b, 1), :].astype(jnp.float32)
@@ -98,6 +115,100 @@
         return 0
 
     lax.fori_loop(0, ACTIVE, block, 0)
+    if do_gw:
+        for n in range(HALF):
+            at = n * PAIR
+            gw_ref[n] = jnp.concatenate(
+                [
+                    sums[CHANNELS:, at : at + PAIR].T[:CHANNELS],
+                    sums[:CHANNELS, at + CHANNELS : at + PAIR],
+                ],
+                axis=1,
+            )
+
+
+def reduce_kernel(
+    x_ref, o_ref, got, terms, whole, send_b, recv_b, send_e, recv_e, send_g, recv_g
+):
+    blk, event = lax.axis_index("blk"), lax.axis_index("event")
+    blks, events = lax.axis_size("blk"), lax.axis_size("event")
+
+    def near(k):
+        return lax.rem(blk + k, blks)
+
+    def far(k):
+        return lax.rem(event + k, events)
+
+    barrier = pltpu.get_barrier_semaphore()
+    for k in range(1, blks):
+        pl.semaphore_signal(
+            barrier, inc=1, device_id=(event, near(k)), device_id_type=pl.DeviceIdType.MESH
+        )
+    for k in range(1, events):
+        pl.semaphore_signal(
+            barrier, inc=1, device_id=(far(k), blk), device_id_type=pl.DeviceIdType.MESH
+        )
+    pl.semaphore_wait(barrier, blks + events - 2)
+
+    def send(src, dst, out_sem, in_sem, target):
+        copy = pltpu.make_async_remote_copy(
+            src_ref=src,
+            dst_ref=dst,
+            send_sem=out_sem,
+            recv_sem=in_sem,
+            device_id=target,
+            device_id_type=pl.DeviceIdType.MESH,
+        )
+        copy.start()
+        return copy
+
+    copies = [
+        send(x_ref.at[near(k)], got.at[k - 1], send_b.at[k], recv_b.at[k], (event, near(k)))
+        for k in range(1, blks)
+    ]
+    total = x_ref[blk]
+    for k, copy in enumerate(copies):
+        copy.wait()
+        total += got[k]
+    terms[event] = total
+    copies = [
+        send(terms.at[event], terms.at[event], send_e.at[k], recv_e.at[k], (far(k), blk))
+        for k in range(1, events)
+    ]
+    for copy in copies:
+        copy.wait()
+    total = terms[0]
+    for k in range(1, events):
+        total += terms[k]
+    whole[blk] = total
+    copies = [
+        send(whole.at[blk], whole.at[blk], send_g.at[k], recv_g.at[k], (event, near(k)))
+        for k in range(1, blks)
+    ]
+    for copy in copies:
+        copy.wait()
+    o_ref[...] = whole[...]
+
+
+def reduced(local):
+    blks, events = lax.axis_size("blk"), lax.axis_size("event")
+    parts = local.reshape(blks, -1, PAIR)
+    vmem = pl.BlockSpec(memory_space=pltpu.VMEM)
+    sems = [pltpu.SemaphoreType.DMA((n,)) for n in (blks, blks, events, events, blks, blks)]
+    total = pl.pallas_call(
+        reduce_kernel,
+        out_shape=jax.ShapeDtypeStruct(parts.shape, parts.dtype),
+        in_specs=[vmem],
+        out_specs=vmem,
+        scratch_shapes=[
+            pltpu.VMEM((blks - 1,) + parts.shape[1:], jnp.float32),
+            pltpu.VMEM((events,) + parts.shape[1:], jnp.float32),
+            pltpu.VMEM(parts.shape, jnp.float32),
+        ]
+        + sems,
+        compiler_params=pltpu.CompilerParams(collective_id=0, has_side_effects=True),
+    )(parts)
+    return total.reshape(local.shape)
 
 
 def run(do_conv, do_gw, cells, x, g, occ, lo, hi, w):
@@ -114,9 +225,12 @@
         shapes += [jax.ShapeDtypeStruct(x.shape, x.dtype)] * 2
         flops += 4 * ACTIVE * VOXELS * TAPS * CHANNELS * PAIR * 2
     if do_gw:
-        shapes.append(jax.ShapeDtypeStruct((PAIR, HALF * PAIR), jnp.float32))
+        shapes.append(jax.ShapeDtypeStruct((HALF, CHANNELS, PAIR), jnp.float32))
         scratch.append(pltpu.VMEM((ACTIVE, PAIR, VOXELS), jnp.bfloat16))
+        scratch.append(pltpu.VMEM((PAIR, HALF * PAIR), jnp.float32))
         flops += 2 * ACTIVE * VOXELS * HALF * PAIR * PAIR * 2
+    if do_conv:
+        scratch.append(pltpu.VMEM((3, 9 * PAIR, PAIR), jnp.bfloat16))
     return pl.pallas_call(
         functools.partial(kernel, do_conv, do_gw),
         out_shape=shapes,
@@ -134,29 +248,22 @@
     half = occ.astype(jnp.bfloat16)
 
     def faces(at):
-        part = jnp.concatenate([x[:, :, at : at + FACE], g[:, :, at : at + FACE]], axis=1)
-        part = part * half[:, None, at : at + FACE]
-        return jnp.transpose(part, (0, 2, 1))
+        span = slice(at, at + FACE)
+        mask = half[:, None, span]
+        return jnp.concatenate([x[:, :, span] * mask, g[:, :, span] * mask], axis=2)
 
     from_below = shifted(faces(VOXELS - FACE), "blk", 1)
     from_above = shifted(faces(0), "blk", -1)
     filler = block_cells[0, :ACTIVE]
     listed = jnp.concatenate([filler, block_cells[0], filler])
     cells = lax.dynamic_slice_in_dim(listed, device * ACTIVE, 3 * ACTIVE).reshape(3, ACTIVE)
-    none = jnp.zeros_like(weight)
-    turned = jnp.transpose(weight[::-1], (0, 2, 1))
-    w = jnp.concatenate(
-        [jnp.concatenate([weight, none], axis=2), jnp.concatenate([none, turned], axis=2)], axis=1
-    ).reshape(3, 9 * PAIR, PAIR)
+    w = weight
     if SPLIT:
         (terms,) = run(False, True, cells, x, g, occ, from_below, from_above, w)
     else:
         output, back, terms = run(True, True, cells, x, g, occ, from_below, from_above, w)
-    terms = terms.reshape(PAIR, HALF, PAIR)
-    upper = jnp.transpose(terms[CHANNELS:, :, :CHANNELS], (1, 2, 0))
-    lower = jnp.transpose(terms[:CHANNELS, :0:-1, CHANNELS:], (1, 0, 2))
-    local = jnp.concatenate([lower, upper], axis=0).reshape(-1, PAIR)
-    grad_weight = lax.psum(local, ("event", "blk")).reshape(TAPS, CHANNELS, CHANNELS)
+    terms = reduced(terms)
+    grad_weight = jnp.concatenate([terms[:0:-1, :, CHANNELS:], terms[:, :, :CHANNELS]], axis=0)
     if SPLIT:
         output, back = run(True, False, cells, x, g, occ, from_below, from_above, w)
     return (output[None], back[None], grad_weight)

time: 222 us -> 96.2 us (0.43)
  waiting for transfers between devices: 137 us -> 3.55 us
  Pallas kernels: 47.7 us -> 81.4 us
  between operations: 14.2 us -> 0.73 us
  local copies, waits for them, and re-layouts: 16.1 us -> 2.87 us
    psum x1 -> x0, waiting for transfers between devices: 137 us -> none  [per_device(): lax.psum(local, ('event', 'blk')).reshape(TAPS, CHANNELS, CHANNELS)]
    pallas_call x0 -> x1, Pallas kernels: none -> 31.6 us  [reduced(): pl.pallas_call(reduce_kernel, out_shape=jax.ShapeDtypeStruct(parts.shape,...]
    unnamed x15 -> x8, local copies, waits for them, and re-layouts: 10.7 us -> 0.77 us
    ppermute x2, waiting for transfers between devices: 0.01 us -> 3.55 us  [shifted(): return lax.ppermute(x, axis, pairs)]
  transfers between devices with their start and end apart: 3 -> 2, of which waited for: 1 -> 1; matrix products, arithmetic and copies ran while one was open for 2% -> 1% of each run, Pallas kernels for 0% -> 0%
where the time goes in v2:
time: 96.2 us
  Pallas kernels  81.4 us (85%)
  other arithmetic  3.98 us (4%)
  starting transfers between devices  3.67 us (4%)
  waiting for transfers between devices  3.55 us (4%)
  local copies, waits for them, and re-layouts  2.87 us (3%)
    pallas_call x1, Pallas kernels, run(): pl.pallas_call(functools.partial(kernel, do_conv, do_gw), out_shape=shape...  49.9 us
    pallas_call x1, Pallas kernels, reduced(): pl.pallas_call(reduce_kernel, out_shape=jax.ShapeDtypeStruct(parts.shape,...  31.6 us
    ppermute x2, starting transfers between devices, shifted(): return lax.ppermute(x, axis, pairs)  3.67 us
    ppermute x2, waiting for transfers between devices, shifted(): return lax.ppermute(x, axis, pairs)  3.55 us
  transfers between devices with their start and end apart: 2, of which 1 were waited for; matrix products, arithmetic and copies ran while one was open for 1% of the time, Pallas kernels for 0%

profile of v2, /device:TPU:0, one launch (start us, length us, event | category | flops | bytes accessed | tf_op | source)
XLA Modules:
  0.0 96.2 jit_solution(14936750648875199049)
XLA Ops:
  0.6 0.8 bitcast_convert_fusion
  1.4 0.1 fusion
  1.5 1.7 %slice_multiply_fusion = (bf16[24,64,64]{2,1,0:T(8,128)(2,1)S(1)}, bf16[24,64,64]{2,1,0:T(8,128)(2,1)S(1)}, bf16[24,64,64]{2,1,0:T(8,128)(2,1)S(1)}, bf16[24,64,64]{2,1,0:T(8,128)(2,1)S(1)}) fusion(bf16[24,64,512]{2,1,0:T(8,128)(2,1)} %bitcast.17, bf16[24,64]{1,0:T(8,128)(2,1)S(1)} %get-tuple-element.13, bf16[24,64]{1,0:T(8,128)(2,1)S(1)} %get-tuple-element.14, ...), kind=kLoop, calls=%fused_computation.1 | loop fusion | flops 393216 | bytes 1579008 | tf_op jit(solution)/shard_map/mul | solution.py:253
  3.2 0.0 copy-start.1
  3.2 0.2 pad_maximum_fusion.1
  3.4 2.4 %collective-permute-start = (bf16[24,64,128]{2,1,0:T(8,128)(2,1)S(1)}, bf16[24,64,128]{2,1,0:T(8,128)(2,1)S(1)}, u32[]{:S(2)}, u32[]{:S(2)}) collective-permute-start(bf16[24,64,128]{2,1,0:T(8,128)(2,1)S(1)} %pad_maximum_fusion.1), channel_id=1, source_target_pairs={{0,1},{1,2},{2,3},{3,4},{4,5},{5,6},{6,7},{8,9},{9,10},{10,11},{11... | collective-permute-start | bytes 1179656 | tf_op jit(solution)/shard_map/ppermute | solution.py:25
  5.8 0.2 pad_maximum_fusion.2
  6.1 1.3 %collective-permute-start.1 = (bf16[24,64,128]{2,1,0:T(8,128)(2,1)S(1)}, bf16[24,64,128]{2,1,0:T(8,128)(2,1)S(1)}, u32[]{:S(2)}, u32[]{:S(2)}) collective-permute-start(bf16[24,64,128]{2,1,0:T(8,128)(2,1)S(1)} %pad_maximum_fusion.2), channel_id=1, source_target_pairs={{1,0},{2,1},{3,2},{4,3},{5,4},{6,5},{7,6},{9,8},{10,9},{11,10},{12... | collective-permute-start | bytes 1179656 | tf_op jit(solution)/shard_map/ppermute | solution.py:25
  7.4 0.0 copy-done.1
  7.4 0.1 pad_add_fusion
  7.5 0.1 dynamic_slice.3
  7.5 0.7 reshape.17.cells
  8.2 0.0 collective-permute-done.lo_ref
  8.2 0.0 copy-start.2
  8.2 3.5 %collective-permute-done.1.hi_ref = bf16[24,64,128]{2,1,0:T(8,128)(2,1)S(1)} collective-permute-done((bf16[24,64,128]{2,1,0:T(8,128)(2,1)S(1)}, bf16[24,64,128]{2,1,0:T(8,128)(2,1)S(1)}, u32[]{:S(2)}, u32[]{:S(2)}) %collective-permute-start.1) | collective-permute-done | bytes 393248 | tf_op jit(solution)/shard_map/ppermute | solution.py:25
  11.8 0.0 copy-start.3
  11.8 0.0 copy-done.2
  11.8 0.8 copy-done.3
  12.5 49.9 %shard_map.76 = (bf16[24,64,512]{2,1,0:T(8,128)(2,1)}, bf16[24,64,512]{2,1,0:T(8,128)(2,1)}, f32[14,64,128]{2,1,0:T(8,128)}) custom-call(s32[3,24]{1,0:T(4,128)} %reshape.17.cells, bf16[24,64,512]{2,1,0:T(8,128)(2,1)} %bitcast.16, bf16[24,64,512]{2,1,0:T(8,128)(2,1)} %bitcast.18, s32[24,512]{1,0:T(8,128)} %bitcast.19, bf16[24,64,128]{2,1,0:T(8,128)(2,1)} %copy-done.2, ...), custom_call_target="tpu_custom_call" | custom-call | flops 33017561088 | bytes 6291456 | tf_op jit(solution)/shard_map/pallas_call | solution.py:234
  62.4 31.6 %shard_map.77 = f32[8,112,128]{2,1,0:T(8,128)} custom-call(f32[8,112,128]{2,1,0:T(8,128)} %bitcast.14), custom_call_target="tpu_custom_call" | custom-call | tf_op jit(solution)/shard_map/pallas_call | solution.py:198
  94.0 0.0 copy-start
  94.0 1.2 %slice.42 = f32[13,64,64]{2,1,0:T(8,128)S(1)} slice(f32[14,64,128]{2,1,0:T(8,128)} %bitcast.12), slice={[1:14], [0:64], [64:128]} | slice | bytes 425984 | tf_op jit(solution)/shard_map/slice | solution.py:266
  95.3 0.0 copy-done
  95.3 1.0 %pad_maximum_fusion = f32[27,64,64]{2,1,0:T(8,128)} fusion(f32[14,64,64]{2,1,0:T(8,128)S(1)} %bitcast.13, f32[13,64,64]{2,1,0:T(8,128)S(1)} %rev.3), kind=kLoop, calls=%fused_computation | loop fusion | flops 110592 | bytes 884736 | tf_op jit(solution)/shard_map/concatenate | solution.py:266
  (2 shorter events, 0.0 us)
Async XLA Ops:
  3.2 4.2 %copy-start.1 = (s32[1,192]{1,0:T(1,128)S(1)}, s32[1,192]{1,0:T(1,128)}, u32[]{:S(2)}) copy-start(s32[1,192]{1,0:T(1,128)} %param.7) | copy-start | bytes 2308
  3.4 4.8 %collective-permute-start = (bf16[24,64,128]{2,1,0:T(8,128)(2,1)S(1)}, bf16[24,64,128]{2,1,0:T(8,128)(2,1)S(1)}, u32[]{:S(2)}, u32[]{:S(2)}) collective-permute-start(bf16[24,64,128]{2,1,0:T(8,128)(2,1)S(1)} %pad_maximum_fusion.1), channel_id=1, source_target_pairs={{0,1},{1,2},{2,3},{3,4},{4,5},{5,6},{6,7},{8,9},{9,10},{10,11},{11... | collective-permute-start | bytes 1179656 | tf_op jit(solution)/shard_map/ppermute | solution.py:25
  6.1 5.7 %collective-permute-start.1 = (bf16[24,64,128]{2,1,0:T(8,128)(2,1)S(1)}, bf16[24,64,128]{2,1,0:T(8,128)(2,1)S(1)}, u32[]{:S(2)}, u32[]{:S(2)}) collective-permute-start(bf16[24,64,128]{2,1,0:T(8,128)(2,1)S(1)} %pad_maximum_fusion.2), channel_id=1, source_target_pairs={{1,0},{2,1},{3,2},{4,3},{5,4},{6,5},{7,6},{9,8},{10,9},{11,10},{12... | collective-permute-start | bytes 1179656 | tf_op jit(solution)/shard_map/ppermute | solution.py:25
  8.2 3.6 %copy-start.2 = (bf16[24,64,128]{2,1,0:T(8,128)(2,1)}, bf16[24,64,128]{2,1,0:T(8,128)(2,1)S(1)}, u32[]{:S(2)}) copy-start(bf16[24,64,128]{2,1,0:T(8,128)(2,1)S(1)} %collective-permute-done.lo_ref) | copy-start | bytes 1179652
  11.8 0.8 copy-start.3
  94.0 1.3 %copy-start = (f32[8,112,128]{2,1,0:T(8,128)S(1)}, f32[8,112,128]{2,1,0:T(8,128)}, u32[]{:S(2)}) copy-start(f32[8,112,128]{2,1,0:T(8,128)} %shard_map.77) | copy-start | bytes 1376260

commit v3 on v1

v3 whole, which is shorter than its diff:
```python
import jax
import jax.numpy as jnp
from jax import lax
from jax.experimental import pallas as pl
from jax.experimental.pallas import tpu as pltpu
from jax.sharding import PartitionSpec as P

CHANNELS = 64
EDGE = 8
VOXELS = 512
FACE = EDGE * EDGE
TAPS = 27
GRID_Y = 8
GRID_Z = 8
ACTIVE = 24
PAIR = 2 * CHANNELS
HALF = TAPS // 2 + 1


def turned(face):
    face = face.astype(jnp.float32)
    return jnp.concatenate([face[:, :FACE], face[:, FACE:]], axis=0).T


def corner(q):
    return lax.div(q, GRID_Z) * EDGE, pl.multiple_of(lax.rem(q, GRID_Z) * EDGE, EDGE)


def kernel(
    slots, cells, x_ref, g_ref, occ_ref, w_ref,
    out_ref, back_ref, gw_ref,
    plane, cols, rows_ref, sums, taps_ref, table, low, high,
    face_lo, face_hi, in_lo, in_hi, flat, parts, got, terms, whole,
    send_b, recv_b, send_e, recv_e, send_g, recv_g, send_f, recv_f,
):
    blk, event = lax.axis_index("blk"), lax.axis_index("event")
    blks, events = lax.axis_size("blk"), lax.axis_size("event")

    def near(k):
        return lax.rem(blk + k, blks)

    def far(k):
        return lax.rem(event + k, events)

    def send(src, dst, out_sem, in_sem, target):
        copy = pltpu.make_async_remote_copy(
            src_ref=src,
            dst_ref=dst,
            send_sem=out_sem,
            recv_sem=in_sem,
            device_id=target,
            device_id_type=pl.DeviceIdType.MESH,
        )
        copy.start()
        return copy

    barrier = pltpu.get_barrier_semaphore()
    for k in range(1, blks):
        pl.semaphore_signal(
            barrier, inc=1, device_id=(event, near(k)), device_id_type=pl.DeviceIdType.MESH
        )
    for k in range(1, events):
        pl.semaphore_signal(
            barrier, inc=1, device_id=(far(k), blk), device_id_type=pl.DeviceIdType.MESH
        )

    def masked(b, span):
        mask = occ_ref[pl.ds(b, 1), :].astype(jnp.float32)[:, span]
        return (
            x_ref[b, :, span].astype(jnp.float32) * mask,
            g_ref[b, :, span].astype(jnp.float32) * mask,
        )

    def make_faces(b, _):
        x, g = masked(b, slice(0, PAIR))
        face_lo[b] = jnp.concatenate([x[:, :FACE], g[:, :FACE]], axis=1).astype(jnp.bfloat16)
        x, g = masked(b, slice(VOXELS - PAIR, VOXELS))
        face_hi[b] = jnp.concatenate([x[:, FACE:], g[:, FACE:]], axis=1).astype(jnp.bfloat16)
        return 0

    lax.fori_loop(0, ACTIVE, make_faces, 0)
    pl.semaphore_wait(barrier, blks + events - 2)
    halo = [
        send(face_hi, in_lo, send_f.at[0], recv_f.at[0], (event, near(1))),
        send(face_lo, in_hi, send_f.at[1], recv_f.at[1], (event, near(blks - 1))),
    ]

    def clear(i, _):
        plane[i, 0] = jnp.zeros(plane.shape[2:], plane.dtype)
        plane[i, GRID_Y * EDGE + 1] = jnp.zeros(plane.shape[2:], plane.dtype)
        edge = jnp.zeros((GRID_Y * EDGE + 2, EDGE, PAIR), plane.dtype)
        plane[i, :, :EDGE, :] = edge
        plane[i, :, (GRID_Z + 1) * EDGE :, :] = edge
        return 0

    lax.fori_loop(0, EDGE + 2, clear, 0)
    sums[...] = jnp.zeros(sums.shape, sums.dtype)
    table[ACTIVE] = jnp.zeros(table.shape[1:], table.dtype)
    low[ACTIVE] = jnp.zeros(low.shape[1:], low.dtype)
    high[ACTIVE] = jnp.zeros(high.shape[1:], high.dtype)
    none = jnp.zeros((CHANNELS, CHANNELS), jnp.float32)
    for t in range(TAPS):
        a, at = t // 9, t % 9 * PAIR
        ahead = w_ref[t].astype(jnp.float32)
        behind = w_ref[TAPS - 1 - t].astype(jnp.float32).T
        taps_ref[a, at : at + CHANNELS] = jnp.concatenate([ahead, none], axis=1).astype(jnp.bfloat16)
        taps_ref[a, at + CHANNELS : at + PAIR] = jnp.concatenate([none, behind], axis=1).astype(
            jnp.bfloat16
        )

    def prepare(b, _):
        both = jnp.concatenate(masked(b, slice(0, VOXELS)), axis=0)
        rows_ref[b] = both.astype(jnp.bfloat16)
        table[b] = both.T
        return 0

    lax.fori_loop(0, ACTIVE, prepare, 0)

    def fill(q, _):
        y, z = corner(q)
        plane[1 : EDGE + 1, pl.ds(y + 1, EDGE), pl.ds(z + EDGE, EDGE), :] = table[
            slots[1, q]
        ].reshape(EDGE, EDGE, EDGE, PAIR)
        return 0

    lax.fori_loop(0, GRID_Y * GRID_Z, fill, 0)
    for copy in halo:
        copy.wait()

    def turn(b, _):
        low[b] = turned(in_lo[b])
        high[b] = turned(in_hi[b])
        return 0

    lax.fori_loop(0, ACTIVE, turn, 0)

    def fill_faces(q, _):
        y, z = corner(q)
        for layer, faces, at in ((0, low, 0), (2, high, EDGE + 1)):
            plane[at, pl.ds(y + 1, EDGE), pl.ds(z + EDGE, EDGE), :] = faces[
                slots[layer, q]
            ].reshape(EDGE, EDGE, PAIR)
        return 0

    lax.fori_loop(0, GRID_Y * GRID_Z, fill_faces, 0)

    def spread(b):
        y, z = cells[0, b] * EDGE, cells[1, b] * EDGE
        for c in range(3):
            for e in range(3):
                part = plane[:, pl.ds(y + c, EDGE), pl.ds(z + EDGE - 1 + e, EDGE), :]
                at = (3 * c + e) * PAIR
                cols[:, at : at + PAIR] = part.reshape((EDGE + 2) * FACE, PAIR).astype(jnp.bfloat16)

    def gradient(b, _):
        spread(b)
        rows = rows_ref[b]
        sums[:, : 5 * PAIR] += jnp.dot(
            rows, cols[FACE : FACE + VOXELS, 4 * PAIR :], preferred_element_type=jnp.float32
        )
        sums[:, 5 * PAIR :] += jnp.dot(
            rows, cols[2 * FACE :, :], preferred_element_type=jnp.float32
        )
        return 0

    def convolve(b, _):
        spread(b)
        total = jnp.dot(cols[:VOXELS, :], taps_ref[0], preferred_element_type=jnp.float32)
        for a in (1, 2):
            total += jnp.dot(
                cols[a * FACE : a * FACE + VOXELS, :],
                taps_ref[a],
                preferred_element_type=jnp.float32,
            )
        mask = occ_ref[pl.ds(b, 1), :].astype(jnp.float32)
        result = (total.T * mask).astype(jnp.bfloat16)
        out_ref[b] = result[:CHANNELS]
        back_ref[b] = result[CHANNELS:]
        return 0

    lax.fori_loop(0, ACTIVE, gradient, 0)
    for n in range(HALF):
        at = n * PAIR
        flat[n * CHANNELS : (n + 1) * CHANNELS] = jnp.concatenate(
            [
                sums[CHANNELS:, at : at + PAIR].T[:CHANNELS],
                sums[:CHANNELS, at + CHANNELS : at + PAIR],
            ],
            axis=1,
        )
    size = parts.shape[1]
    for k in range(blks):
        parts[k] = flat[k * size : (k + 1) * size]

    third = ACTIVE // 3
    copies = [
        send(parts.at[near(k)], got.at[k - 1], send_b.at[k], recv_b.at[k], (event, near(k)))
        for k in range(1, blks)
    ]
    lax.fori_loop(0, third, convolve, 0)
    total = parts[blk]
    for k, copy in enumerate(copies):
        copy.wait()
        total += got[k]
    terms[event] = total
    copies = [
        send(terms.at[event], terms.at[event], send_e.at[k], recv_e.at[k], (far(k), blk))
        for k in range(1, events)
    ]
    lax.fori_loop(third, 2 * third, convolve, 0)
    for copy in copies:
        copy.wait()
    total = terms[0]
    for k in range(1, events):
        total += terms[k]
    whole[blk] = total
    copies = [
        send(whole.at[blk], whole.at[blk], send_g.at[k], recv_g.at[k], (event, near(k)))
        for k in range(1, blks)
    ]
    lax.fori_loop(2 * third, ACTIVE, convolve, 0)
    for copy in copies:
        copy.wait()
    gw_ref[...] = whole[...]


def per_device(features, occupancy, block_cells, weight, cotangent):
    device = lax.axis_index("blk")
    blks, events = lax.axis_size("blk"), lax.axis_size("event")
    x, g, occ = features[0], cotangent[0], occupancy[0]
    planes = block_cells[0].reshape(blks, ACTIVE)
    hits = planes[:, None, :] == jnp.arange(GRID_Y * GRID_Z, dtype=jnp.int32)[None, :, None]
    listing = jnp.arange(ACTIVE, dtype=jnp.int32) - ACTIVE
    slots = ACTIVE + jnp.sum(jnp.where(hits, listing, 0), axis=-1)
    slots = jnp.pad(slots, ((1, 1), (0, 0)), constant_values=ACTIVE)
    slots = lax.dynamic_slice_in_dim(slots, device, 3).astype(jnp.int32)
    cells = lax.dynamic_slice_in_dim(block_cells[0], device * ACTIVE, ACTIVE)
    cells = jnp.stack([lax.div(cells, GRID_Z), lax.rem(cells, GRID_Z)])
    part = (HALF * CHANNELS // blks, PAIR)
    vmem = pl.BlockSpec(memory_space=pltpu.VMEM)
    smem = pl.BlockSpec(memory_space=pltpu.SMEM)
    wide, half = jnp.float32, jnp.bfloat16
    face = (ACTIVE, CHANNELS, PAIR)
    output, back, terms = pl.pallas_call(
        kernel,
        out_shape=[
            jax.ShapeDtypeStruct(x.shape, x.dtype),
            jax.ShapeDtypeStruct(x.shape, x.dtype),
            jax.ShapeDtypeStruct((blks,) + part, wide),
        ],
        in_specs=[smem, smem, vmem, vmem, vmem, vmem],
        out_specs=[vmem] * 3,
        scratch_shapes=[
            pltpu.VMEM((EDGE + 2, GRID_Y * EDGE + 2, (GRID_Z + 2) * EDGE, PAIR), wide),
            pltpu.VMEM(((EDGE + 2) * FACE, 9 * PAIR), half),
            pltpu.VMEM((ACTIVE, PAIR, VOXELS), half),
            pltpu.VMEM((PAIR, HALF * PAIR), wide),
            pltpu.VMEM((3, 9 * PAIR, PAIR), half),
            pltpu.VMEM((ACTIVE + 1, VOXELS, PAIR), wide),
            pltpu.VMEM((ACTIVE + 1, FACE, PAIR), wide),
            pltpu.VMEM((ACTIVE + 1, FACE, PAIR), wide),
            pltpu.VMEM(face, half),
            pltpu.VMEM(face, half),
            pltpu.VMEM(face, half),
            pltpu.VMEM(face, half),
            pltpu.VMEM((HALF * CHANNELS, PAIR), wide),
            pltpu.VMEM((blks,) + part, wide),
            pltpu.VMEM((blks - 1,) + part, wide),
            pltpu.VMEM((events,) + part, wide),
            pltpu.VMEM((blks,) + part, wide),
        ]
        + [
            pltpu.SemaphoreType.DMA((n,))
            for n in (blks, blks, events, events, blks, blks, 2, 2)
        ],
        cost_estimate=pl.CostEstimate(
            flops=2 * ACTIVE * VOXELS * TAPS * CHANNELS * CHANNELS * 3,
            bytes_accessed=8 * x.size,
            transcendentals=0,
        ),
        compiler_params=pltpu.CompilerParams(
            vmem_limit_bytes=58 * 1024 * 1024, collective_id=0, has_side_effects=True
        ),
    )(slots, cells, x, g, occ, weight)
    terms = terms.reshape(HALF, CHANNELS, PAIR)
    grad_weight = jnp.concatenate([terms[:0:-1, :, CHANNELS:], terms[:, :, :CHANNELS]], axis=0)
    return (output[None], back[None], grad_weight)


def solution(mesh):
    in_specs = (
        P("event", "blk", None, None),
        P("event", "blk", None),
        P("event", None),
        P(),
        P("event", "blk", None, None),
    )
    out_specs = (P("event", "blk", None, None), P("event", "blk", None, None), P())
    return jax.shard_map(
        per_device, mesh=mesh, in_specs=in_specs, out_specs=out_specs, check_vma=False
    )
```

time: 222 us -> 77.3 us (0.35)
  waiting for transfers between devices: 137 us -> 0 us
  Pallas kernels: 47.7 us -> 66.8 us
  between operations: 14.2 us -> 0.7 us
  local copies, waits for them, and re-layouts: 16.1 us -> 5.66 us
  starting transfers between devices: 4.38 us -> 0 us
    psum x1 -> x0, waiting for transfers between devices: 137 us -> none  [per_device(): lax.psum(local, ('event', 'blk')).reshape(TAPS, CHANNELS, CHANNELS)]
    pallas_call x1, Pallas kernels: 47.7 us -> 66.8 us  [per_device(): pl.pallas_call(kernel, out_shape=[jax.ShapeDtypeStruct(x.shape, x.dtype),...]
    unnamed x15 -> x9, local copies, waits for them, and re-layouts: 10.7 us -> 3.64 us
    ppermute x2 -> x0, starting transfers between devices: 4.35 us -> none  [shifted(): return lax.ppermute(x, axis, pairs)]
  transfers between devices with their start and end apart: 3 -> 0, of which waited for: 1 -> 0; matrix products, arithmetic and copies ran while one was open for 2% -> 0% of each run, Pallas kernels for 0% -> 0%
where the time goes in v3:
time: 77.3 us; the launch traced here: 77 us
  Pallas kernels  66.8 us (86%)
  local copies, waits for them, and re-layouts  5.66 us (7%)
  other arithmetic  3.77 us (5%)
    pallas_call x1, Pallas kernels, per_device(): pl.pallas_call(kernel, out_shape=[jax.ShapeDtypeStruct(x.shape, x.dtype),...  66.8 us
    unnamed x9, local copies, waits for them, and re-layouts  3.64 us

profile of v3, /device:TPU:0, one launch (start us, length us, event | category | flops | bytes accessed | tf_op | source)
XLA Modules:
  0.0 77.0 jit_solution(9757633439459598721)
XLA Ops:
  0.6 0.5 broadcast.20
  1.1 1.3 %reduce.3 = s32[192]{0:T(256)S(1)} reduce(s32[1,192]{1,0:T(1,128)} %param.7, s32[]{:T(128)} %broadcast.20), dimensions={0}, to_apply=%param.7.reduce_sub_computation.3 | reduce | bytes 1540 | tf_op args[2]
  2.5 0.8 compare_select_fusion.1
  3.3 0.6 pad_add_fusion.cells
  3.8 0.1 eq.15
  3.9 0.1 select_reduce_fusion
  4.0 0.6 pad_dynamic-slice_fusion.slots
  4.6 66.8 %shard_map.76 = (bf16[24,64,512]{2,1,0:T(8,128)(2,1)}, bf16[24,64,512]{2,1,0:T(8,128)(2,1)}, f32[8,112,128]{2,1,0:T(8,128)}) custom-call(s32[3,64]{1,0:T(4,128)} %pad_dynamic-slice_fusion.slots, s32[2,24]{1,0:T(2,128)} %pad_add_fusion.cells, bf16[24,64,512]{2,1,0:T(8,128)(2,1)} %bitcast.11, bf16[24,64,512]{2,1,0:T(8,128)(2,1)} %bitcast.12, ...), custom_call_target="tpu_custom_call" | custom-call | flops 8153726976 | bytes 6291456 | tf_op jit(solution)/shard_map/pallas_call | solution.py:244
  71.5 0.0 copy-start
  71.5 0.0 copy-start.2
  71.5 1.3 %slice.8 = f32[13,64,64]{2,1,0:T(8,128)S(1)} slice(f32[14,64,128]{2,1,0:T(8,128)} %bitcast.7), slice={[1:14], [0:64], [64:128]} | slice | bytes 425984 | tf_op jit(solution)/shard_map/slice | solution.py:286
  72.9 0.0 copy-done
  72.9 1.0 %pad_maximum_fusion = f32[27,64,64]{2,1,0:T(8,128)} fusion(f32[14,64,64]{2,1,0:T(8,128)S(1)} %bitcast.8, f32[13,64,64]{2,1,0:T(8,128)S(1)} %rev.3), kind=kLoop, calls=%fused_computation | loop fusion | flops 110592 | bytes 884736 | tf_op jit(solution)/shard_map/concatenate | solution.py:286
  73.8 0.0 copy-done.2
  73.8 0.0 copy-start.1
  73.8 1.1 %copy.10 = bf16[1,24,64,512]{3,2,1,0:T(8,128)(2,1)} copy(bf16[1,24,64,512]{3,2,1,0:T(8,128)(2,1)S(1)} %bitcast.10) | data formatting | bytes 3145728
  75.0 0.8 %copy-done.1 = bf16[24,64,512]{2,1,0:T(8,128)(2,1)S(1)} copy-done((bf16[24,64,512]{2,1,0:T(8,128)(2,1)S(1)}, bf16[24,64,512]{2,1,0:T(8,128)(2,1)}, u32[]{:S(2)}) %copy-start.1) | copy-done | bytes 1572888
  75.8 1.1 %copy.11 = bf16[1,24,64,512]{3,2,1,0:T(8,128)(2,1)} copy(bf16[1,24,64,512]{3,2,1,0:T(8,128)(2,1)S(1)} %bitcast.9) | data formatting | bytes 3145728
  (3 shorter events, 0.0 us)
Async XLA Ops:
  71.5 1.4 %copy-start = (f32[8,112,128]{2,1,0:T(8,128)S(1)}, f32[8,112,128]{2,1,0:T(8,128)}, u32[]{:S(2)}) copy-start(f32[8,112,128]{2,1,0:T(8,128)} %get-tuple-element.8) | copy-start | bytes 1376260
  71.5 2.4 %copy-start.2 = (bf16[24,64,512]{2,1,0:T(8,128)(2,1)S(1)}, bf16[24,64,512]{2,1,0:T(8,128)(2,1)}, u32[]{:S(2)}) copy-start(bf16[24,64,512]{2,1,0:T(8,128)(2,1)} %get-tuple-element.6) | copy-start | bytes 4718596
  73.8 2.0 %copy-start.1 = (bf16[24,64,512]{2,1,0:T(8,128)(2,1)S(1)}, bf16[24,64,512]{2,1,0:T(8,128)(2,1)}, u32[]{:S(2)}) copy-start(bf16[24,64,512]{2,1,0:T(8,128)(2,1)} %get-tuple-element.7) | copy-start | bytes 4718596

commit v4 on v3

--- a/solution.py
+++ b/solution.py
@@ -103,8 +103,9 @@
         a, at = t // 9, t % 9 * PAIR
         ahead = w_ref[t].astype(jnp.float32)
         behind = w_ref[TAPS - 1 - t].astype(jnp.float32).T
-        taps_ref[a, at : at + CHANNELS] = jnp.concatenate([ahead, none], axis=1).astype(jnp.bfloat16)
-        taps_ref[a, at + CHANNELS : at + PAIR] = jnp.concatenate([none, behind], axis=1).astype(
+        to = slice(a * PAIR, (a + 1) * PAIR)
+        taps_ref[at : at + CHANNELS, to] = jnp.concatenate([ahead, none], axis=1).astype(jnp.bfloat16)
+        taps_ref[at + CHANNELS : at + PAIR, to] = jnp.concatenate([none, behind], axis=1).astype(
             jnp.bfloat16
         )
 
@@ -165,13 +166,13 @@
 
     def convolve(b, _):
         spread(b)
-        total = jnp.dot(cols[:VOXELS, :], taps_ref[0], preferred_element_type=jnp.float32)
-        for a in (1, 2):
-            total += jnp.dot(
-                cols[a * FACE : a * FACE + VOXELS, :],
-                taps_ref[a],
-                preferred_element_type=jnp.float32,
-            )
+        double = jnp.dot(
+            cols[: VOXELS + FACE, :], taps_ref[:, : 2 * PAIR], preferred_element_type=jnp.float32
+        )
+        total = double[:VOXELS, :PAIR] + double[FACE:, PAIR:]
+        total += jnp.dot(
+            cols[2 * FACE :, :], taps_ref[:, 2 * PAIR :], preferred_element_type=jnp.float32
+        )
         mask = occ_ref[pl.ds(b, 1), :].astype(jnp.float32)
         result = (total.T * mask).astype(jnp.bfloat16)
         out_ref[b] = result[:CHANNELS]
@@ -255,7 +256,7 @@
             pltpu.VMEM(((EDGE + 2) * FACE, 9 * PAIR), half),
             pltpu.VMEM((ACTIVE, PAIR, VOXELS), half),
             pltpu.VMEM((PAIR, HALF * PAIR), wide),
-            pltpu.VMEM((3, 9 * PAIR, PAIR), half),
+            pltpu.VMEM((9 * PAIR, 3 * PAIR), half),
             pltpu.VMEM((ACTIVE + 1, VOXELS, PAIR), wide),
             pltpu.VMEM((ACTIVE + 1, FACE, PAIR), wide),
             pltpu.VMEM((ACTIVE + 1, FACE, PAIR), wide),

time: 77.3 us -> 72.3 us (0.935)
  Pallas kernels: 66.8 us -> 61.8 us
    pallas_call x1, Pallas kernels: 66.8 us -> 61.8 us  [per_device(): pl.pallas_call(kernel, out_shape=[jax.ShapeDtypeStruct(x.shape, x.dtype),...]
where the time goes in v4:
time: 72.3 us; the launch traced here: 72 us
  Pallas kernels  61.8 us (85%)
  local copies, waits for them, and re-layouts  5.66 us (8%)
  other arithmetic  3.77 us (5%)
    pallas_call x1, Pallas kernels, per_device(): pl.pallas_call(kernel, out_shape=[jax.ShapeDtypeStruct(x.shape, x.dtype),...  61.8 us
    unnamed x9, local copies, waits for them, and re-layouts  3.64 us

profile of v4, /device:TPU:0, one launch (start us, length us, event | category | flops | bytes accessed | tf_op | source)
XLA Modules:
  0.0 72.0 jit_solution(17992400347676006418)
XLA Ops:
  0.6 0.5 broadcast.20
  1.1 1.3 %reduce.3 = s32[192]{0:T(256)S(1)} reduce(s32[1,192]{1,0:T(1,128)} %param.7, s32[]{:T(128)} %broadcast.20), dimensions={0}, to_apply=%param.7.reduce_sub_computation.3 | reduce | bytes 1540 | tf_op args[2]
  2.5 0.8 %compare_select_fusion.1 = (s32[1,24]{1,0:T(1,128)S(1)}, s32[1,24]{1,0:T(1,128)S(1)}) fusion(s32[1,192]{1,0:T(1,128)} %param.7, s32[]{:T(128)S(6)} %select_n.12), kind=kLoop, calls=%fused_computation.6 | loop fusion | flops 216 | bytes 292 | tf_op jit(solution)/shard_map/div | solution.py:239
  3.3 0.6 pad_add_fusion.cells
  3.8 0.1 eq.15
  3.9 0.1 select_reduce_fusion
  4.0 0.6 pad_dynamic-slice_fusion.slots
  4.6 61.8 %shard_map.76 = (bf16[24,64,512]{2,1,0:T(8,128)(2,1)}, bf16[24,64,512]{2,1,0:T(8,128)(2,1)}, f32[8,112,128]{2,1,0:T(8,128)}) custom-call(s32[3,64]{1,0:T(4,128)} %pad_dynamic-slice_fusion.slots, s32[2,24]{1,0:T(2,128)} %pad_add_fusion.cells, bf16[24,64,512]{2,1,0:T(8,128)(2,1)} %bitcast.11, bf16[24,64,512]{2,1,0:T(8,128)(2,1)} %bitcast.12, ...), custom_call_target="tpu_custom_call" | custom-call | flops 8153726976 | bytes 6291456 | tf_op jit(solution)/shard_map/pallas_call | solution.py:245
  66.5 0.0 copy-start
  66.5 0.0 copy-start.2
  66.5 1.3 %slice.8 = f32[13,64,64]{2,1,0:T(8,128)S(1)} slice(f32[14,64,128]{2,1,0:T(8,128)} %bitcast.7), slice={[1:14], [0:64], [64:128]} | slice | bytes 425984 | tf_op jit(solution)/shard_map/slice | solution.py:287
  67.8 0.0 copy-done
  67.9 1.0 %pad_maximum_fusion = f32[27,64,64]{2,1,0:T(8,128)} fusion(f32[14,64,64]{2,1,0:T(8,128)S(1)} %bitcast.8, f32[13,64,64]{2,1,0:T(8,128)S(1)} %rev.3), kind=kLoop, calls=%fused_computation | loop fusion | flops 110592 | bytes 884736 | tf_op jit(solution)/shard_map/concatenate | solution.py:287
  68.8 0.0 copy-done.2
  68.8 0.0 copy-start.1
  68.8 1.1 %copy.10 = bf16[1,24,64,512]{3,2,1,0:T(8,128)(2,1)} copy(bf16[1,24,64,512]{3,2,1,0:T(8,128)(2,1)S(1)} %bitcast.10) | data formatting | bytes 3145728
  70.0 0.8 %copy-done.1 = bf16[24,64,512]{2,1,0:T(8,128)(2,1)S(1)} copy-done((bf16[24,64,512]{2,1,0:T(8,128)(2,1)S(1)}, bf16[24,64,512]{2,1,0:T(8,128)(2,1)}, u32[]{:S(2)}) %copy-start.1) | copy-done | bytes 1572888
  70.8 1.1 %copy.11 = bf16[1,24,64,512]{3,2,1,0:T(8,128)(2,1)} copy(bf16[1,24,64,512]{3,2,1,0:T(8,128)(2,1)S(1)} %bitcast.9) | data formatting | bytes 3145728
  (3 shorter events, 0.0 us)
Async XLA Ops:
  66.5 1.4 %copy-start = (f32[8,112,128]{2,1,0:T(8,128)S(1)}, f32[8,112,128]{2,1,0:T(8,128)}, u32[]{:S(2)}) copy-start(f32[8,112,128]{2,1,0:T(8,128)} %get-tuple-element.8) | copy-start | bytes 1376260
  66.5 2.4 %copy-start.2 = (bf16[24,64,512]{2,1,0:T(8,128)(2,1)S(1)}, bf16[24,64,512]{2,1,0:T(8,128)(2,1)}, u32[]{:S(2)}) copy-start(bf16[24,64,512]{2,1,0:T(8,128)(2,1)} %get-tuple-element.6) | copy-start | bytes 4718596
  68.8 2.0 %copy-start.1 = (bf16[24,64,512]{2,1,0:T(8,128)(2,1)S(1)}, bf16[24,64,512]{2,1,0:T(8,128)(2,1)}, u32[]{:S(2)}) copy-start(bf16[24,64,512]{2,1,0:T(8,128)(2,1)} %get-tuple-element.7) | copy-start | bytes 4718596

commit v5 on v4

--- a/solution.py
+++ b/solution.py
@@ -145,7 +145,7 @@
 
     lax.fori_loop(0, GRID_Y * GRID_Z, fill_faces, 0)
 
-    def spread(b):
+    def spread(b, cols):
         y, z = cells[0, b] * EDGE, cells[1, b] * EDGE
         for c in range(3):
             for e in range(3):
@@ -153,8 +153,7 @@
                 at = (3 * c + e) * PAIR
                 cols[:, at : at + PAIR] = part.reshape((EDGE + 2) * FACE, PAIR).astype(jnp.bfloat16)
 
-    def gradient(b, _):
-        spread(b)
+    def gradient(b, cols):
         rows = rows_ref[b]
         sums[:, : 5 * PAIR] += jnp.dot(
             rows, cols[FACE : FACE + VOXELS, 4 * PAIR :], preferred_element_type=jnp.float32
@@ -162,10 +161,8 @@
         sums[:, 5 * PAIR :] += jnp.dot(
             rows, cols[2 * FACE :, :], preferred_element_type=jnp.float32
         )
-        return 0
-
-    def convolve(b, _):
-        spread(b)
+
+    def convolve(b, cols):
         double = jnp.dot(
             cols[: VOXELS + FACE, :], taps_ref[:, : 2 * PAIR], preferred_element_type=jnp.float32
         )
@@ -177,9 +174,18 @@
         result = (total.T * mask).astype(jnp.bfloat16)
         out_ref[b] = result[:CHANNELS]
         back_ref[b] = result[CHANNELS:]
-        return 0
-
-    lax.fori_loop(0, ACTIVE, gradient, 0)
+
+    def paired(work, start, stop):
+        def step(i, _):
+            spread(2 * i, cols.at[0])
+            spread(2 * i + 1, cols.at[1])
+            work(2 * i, cols.at[0])
+            work(2 * i + 1, cols.at[1])
+            return 0
+
+        lax.fori_loop(start // 2, stop // 2, step, 0)
+
+    paired(gradient, 0, ACTIVE)
     for n in range(HALF):
         at = n * PAIR
         flat[n * CHANNELS : (n + 1) * CHANNELS] = jnp.concatenate(
@@ -198,7 +204,7 @@
         send(parts.at[near(k)], got.at[k - 1], send_b.at[k], recv_b.at[k], (event, near(k)))
         for k in range(1, blks)
     ]
-    lax.fori_loop(0, third, convolve, 0)
+    paired(convolve, 0, third)
     total = parts[blk]
     for k, copy in enumerate(copies):
         copy.wait()
@@ -208,7 +214,7 @@
         send(terms.at[event], terms.at[event], send_e.at[k], recv_e.at[k], (far(k), blk))
         for k in range(1, events)
     ]
-    lax.fori_loop(third, 2 * third, convolve, 0)
+    paired(convolve, third, 2 * third)
     for copy in copies:
         copy.wait()
     total = terms[0]
@@ -219,7 +225,7 @@
         send(whole.at[blk], whole.at[blk], send_g.at[k], recv_g.at[k], (event, near(k)))
         for k in range(1, blks)
     ]
-    lax.fori_loop(2 * third, ACTIVE, convolve, 0)
+    paired(convolve, 2 * third, ACTIVE)
     for copy in copies:
         copy.wait()
     gw_ref[...] = whole[...]
@@ -253,7 +259,7 @@
         out_specs=[vmem] * 3,
         scratch_shapes=[
             pltpu.VMEM((EDGE + 2, GRID_Y * EDGE + 2, (GRID_Z + 2) * EDGE, PAIR), wide),
-            pltpu.VMEM(((EDGE + 2) * FACE, 9 * PAIR), half),
+            pltpu.VMEM((2, (EDGE + 2) * FACE, 9 * PAIR), half),
             pltpu.VMEM((ACTIVE, PAIR, VOXELS), half),
             pltpu.VMEM((PAIR, HALF * PAIR), wide),
             pltpu.VMEM((9 * PAIR, 3 * PAIR), half),

time: 72.3 us -> 66.6 us (0.921)
  Pallas kernels: 61.8 us -> 56.3 us
    pallas_call x1, Pallas kernels: 61.8 us -> 56.3 us  [per_device(): pl.pallas_call(kernel, out_shape=[jax.ShapeDtypeStruct(x.shape, x.dtype),...]
where the time goes in v5:
time: 66.6 us; the launch traced here: 66.5 us
  Pallas kernels  56.3 us (85%)
  local copies, waits for them, and re-layouts  5.66 us (8%)
  other arithmetic  3.77 us (6%)
  between operations  0.7 us (1%)
    pallas_call x1, Pallas kernels, per_device(): pl.pallas_call(kernel, out_shape=[jax.ShapeDtypeStruct(x.shape, x.dtype),...  56.3 us
    unnamed x9, local copies, waits for them, and re-layouts  3.64 us
    unnamed x1, other arithmetic  1.34 us

profile of v5, /device:TPU:0, one launch (start us, length us, event | category | flops | bytes accessed | tf_op | source)
XLA Modules:
  0.0 66.5 jit_solution(73289160759681781)
XLA Ops:
  0.6 0.5 broadcast.20
  1.1 1.3 %reduce.3 = s32[192]{0:T(256)S(1)} reduce(s32[1,192]{1,0:T(1,128)} %param.7, s32[]{:T(128)} %broadcast.20), dimensions={0}, to_apply=%param.7.reduce_sub_computation.3 | reduce | bytes 1540 | tf_op args[2]
  2.5 0.8 %compare_select_fusion.1 = (s32[1,24]{1,0:T(1,128)S(1)}, s32[1,24]{1,0:T(1,128)S(1)}) fusion(s32[1,192]{1,0:T(1,128)} %param.7, s32[]{:T(128)S(6)} %select_n.12), kind=kLoop, calls=%fused_computation.6 | loop fusion | flops 216 | bytes 292 | tf_op jit(solution)/shard_map/div | solution.py:245
  3.3 0.6 pad_add_fusion.cells
  3.8 0.1 eq.15
  3.9 0.1 select_reduce_fusion
  4.0 0.6 pad_dynamic-slice_fusion.slots
  4.6 56.3 %shard_map.76 = (bf16[24,64,512]{2,1,0:T(8,128)(2,1)}, bf16[24,64,512]{2,1,0:T(8,128)(2,1)}, f32[8,112,128]{2,1,0:T(8,128)}) custom-call(s32[3,64]{1,0:T(4,128)} %pad_dynamic-slice_fusion.slots, s32[2,24]{1,0:T(2,128)} %pad_add_fusion.cells, bf16[24,64,512]{2,1,0:T(8,128)(2,1)} %bitcast.11, bf16[24,64,512]{2,1,0:T(8,128)(2,1)} %bitcast.12, ...), custom_call_target="tpu_custom_call" | custom-call | flops 8153726976 | bytes 6291456 | tf_op jit(solution)/shard_map/pallas_call | solution.py:251
  61.0 0.0 copy-start
  61.0 0.0 copy-start.2
  61.0 1.3 %slice.8 = f32[13,64,64]{2,1,0:T(8,128)S(1)} slice(f32[14,64,128]{2,1,0:T(8,128)} %bitcast.7), slice={[1:14], [0:64], [64:128]} | slice | bytes 425984 | tf_op jit(solution)/shard_map/slice | solution.py:293
  62.3 0.0 copy-done
  62.4 1.0 %pad_maximum_fusion = f32[27,64,64]{2,1,0:T(8,128)} fusion(f32[14,64,64]{2,1,0:T(8,128)S(1)} %bitcast.8, f32[13,64,64]{2,1,0:T(8,128)S(1)} %rev.3), kind=kLoop, calls=%fused_computation | loop fusion | flops 110592 | bytes 884736 | tf_op jit(solution)/shard_map/concatenate | solution.py:293
  63.3 0.0 copy-done.2
  63.3 0.0 copy-start.1
  63.3 1.1 %copy.10 = bf16[1,24,64,512]{3,2,1,0:T(8,128)(2,1)} copy(bf16[1,24,64,512]{3,2,1,0:T(8,128)(2,1)S(1)} %bitcast.10) | data formatting | bytes 3145728
  64.5 0.8 %copy-done.1 = bf16[24,64,512]{2,1,0:T(8,128)(2,1)S(1)} copy-done((bf16[24,64,512]{2,1,0:T(8,128)(2,1)S(1)}, bf16[24,64,512]{2,1,0:T(8,128)(2,1)}, u32[]{:S(2)}) %copy-start.1) | copy-done | bytes 1572888
  65.3 1.1 %copy.11 = bf16[1,24,64,512]{3,2,1,0:T(8,128)(2,1)} copy(bf16[1,24,64,512]{3,2,1,0:T(8,128)(2,1)S(1)} %bitcast.9) | data formatting | bytes 3145728
  (3 shorter events, 0.0 us)
Async XLA Ops:
  61.0 1.4 %copy-start = (f32[8,112,128]{2,1,0:T(8,128)S(1)}, f32[8,112,128]{2,1,0:T(8,128)}, u32[]{:S(2)}) copy-start(f32[8,112,128]{2,1,0:T(8,128)} %get-tuple-element.8) | copy-start | bytes 1376260
  61.0 2.4 %copy-start.2 = (bf16[24,64,512]{2,1,0:T(8,128)(2,1)S(1)}, bf16[24,64,512]{2,1,0:T(8,128)(2,1)}, u32[]{:S(2)}) copy-start(bf16[24,64,512]{2,1,0:T(8,128)(2,1)} %get-tuple-element.6) | copy-start | bytes 4718596
  63.3 2.0 %copy-start.1 = (bf16[24,64,512]{2,1,0:T(8,128)(2,1)S(1)}, bf16[24,64,512]{2,1,0:T(8,128)(2,1)}, u32[]{:S(2)}) copy-start(bf16[24,64,512]{2,1,0:T(8,128)(2,1)} %get-tuple-element.7) | copy-start | bytes 4718596
